TPU v7x, 256 devices: a whole 4x4x8 slice. The times are simulated.
256 devices in a mesh: dp: 8 (over y, core), fsdp: 32 (over x, z).
Axes of the slice: x: 4, y: 4, z: 8, core: 2. Of those that a mesh axis runs over, the one named last changes fastest.
Arguments:
- tokens: bfloat16 [32768, 4096], P(('dp', 'fsdp')), may hold values from -18 to 18
- upstream: bfloat16 [32768, 1024], P(('dp', 'fsdp')), may hold values from -6 to 6
- weight: bfloat16 [4096, 1024], P('fsdp'), may hold values from -0.09375 to 0.09375
- owner_table: int32 [16], replicated, may hold values from 0 to 15, as said below
- stats_prev: float32 [32, 512, 512], P('fsdp'), may hold values from -589824 to 1207959552, as said below
- roots_prev: float32 [32, 512, 512], P('fsdp'), may hold values from -1 to 1.1, as said below
Outputs:
- projected: bfloat16 [32768, 1024], P(('dp', 'fsdp'))
- input_grad: bfloat16 [32768, 4096], P(('dp', 'fsdp'))
- roots_next: float32 [32, 512, 512], P('fsdp')
- direction: bfloat16 [4096, 1024], P('fsdp', 'dp')
Inputs may be any that keep to these rules, and one draw needn't show every extreme that they name: `owner_table`: each of the 16 blocks appears once, and entry 0 holds block 0. `stats_prev`: each entry is symmetric and positive definite. `roots_prev`: each entry is symmetric with eigenvalues between 0.7 and 1.1.
All inputs are finite; a program needn't handle non-finite values.
Results may differ from a plain program's by a relative error of at most 0.001.
Values may be sent and summed in bfloat16 or wider, within the bound.
A program may use at most 128 MiB of HBM per device.

v0:
```python
import jax
import jax.numpy as jnp
from jax import lax
from jax.sharding import PartitionSpec as P

HIGHEST = lax.Precision.HIGHEST
STAT_DECAY = 0.8
NORM_EPSILON = 1e-06


def partner(x, axis, stride):
    return lax.ppermute(x, axis, [(i, i ^ 1 << stride) for i in range(lax.axis_size(axis))])


def batched(left, right):
    return jnp.einsum("sij,sjk->sik", left, right, precision=HIGHEST)


def grad_rows(
    tokens,
    upstream,
    owner_table,
    owner_dev,
    local_row,
    unit_rows,
    slot_count,
    half_rows,
    block_size,
):
    col_blocks = upstream.shape[1] // block_size
    slot_index = local_row // half_rows
    offset = local_row % half_rows
    table_entry = owner_dev // 2 * slot_count + slot_index
    chosen = lax.dynamic_index_in_dim(owner_table, table_entry, 0, keepdims=False)
    row_start = chosen // col_blocks * block_size + owner_dev % 2 * half_rows + offset
    col_start = chosen % col_blocks * block_size
    token_cols = lax.dynamic_slice_in_dim(tokens, row_start, unit_rows, 1)
    upstream_cols = lax.dynamic_slice_in_dim(upstream, col_start, block_size, 1)
    return lax.dot_general(
        token_cols, upstream_cols, (((0,), (0,)), ((), ())), preferred_element_type=jnp.float32
    )


def local(tokens, upstream, weight, owner_table, stats_prev, roots_prev):
    kv_width = upstream.shape[1]
    slot_count = stats_prev.shape[0]
    block_size = stats_prev.shape[1]
    half_rows = block_size // 2
    replica_count = lax.axis_size("dp")
    own_rows = slot_count * half_rows
    shard_rows = lax.all_gather(weight, "fsdp", axis=0, tiled=True)
    key_total = jnp.dot(tokens, shard_rows, preferred_element_type=jnp.float32)
    data_part = lax.dot_general(
        upstream, shard_rows, (((1,), (1,)), ((), ())), preferred_element_type=jnp.float32
    )
    input_total = data_part
    key_total, input_total = (key_total, input_total)
    projected = key_total.astype(jnp.bfloat16)
    input_grad = input_total.astype(jnp.bfloat16)

    def unit_term(step_index):
        flat_row = step_index * half_rows
        owner_dev = flat_row // own_rows
        local_row = flat_row % own_rows
        return grad_rows(
            tokens,
            upstream,
            owner_table,
            owner_dev,
            local_row,
            half_rows,
            slot_count,
            half_rows,
            block_size,
        )

    term_rows = lax.map(
        unit_term, jnp.arange(own_rows * lax.axis_size("fsdp") // half_rows, dtype=jnp.int32)
    )
    partial_sum = lax.psum_scatter(
        term_rows.reshape(own_rows * lax.axis_size("fsdp"), block_size),
        "fsdp",
        scatter_dimension=0,
        tiled=True,
    )
    summed = lax.psum(partial_sum, "dp")
    own_half = summed.reshape(slot_count, half_rows, block_size)
    other_half = partner(own_half, "fsdp", 0)
    side_bit = lax.axis_index("fsdp") % 2
    is_left = side_bit == 0
    top_half = jnp.where(is_left, own_half, other_half)
    bottom = jnp.where(is_left, other_half, own_half)
    grad_block = jnp.concatenate([top_half, bottom], axis=1)
    chosen = jnp.where(is_left, grad_block, jnp.swapaxes(grad_block, 1, 2))
    gram_matrix = batched(chosen, jnp.swapaxes(chosen, 1, 2))
    stats = STAT_DECAY * stats_prev + (1.0 - STAT_DECAY) * gram_matrix
    trace_mean = jnp.trace(stats, axis1=1, axis2=2) / block_size
    normed = stats / trace_mean[:, None, None]
    identity = jnp.eye(block_size, dtype=jnp.float32)
    square = batched(roots_prev, roots_prev)
    moment = batched(batched(square, square), normed)
    factor = (5.0 * identity - moment) * 0.25
    iterate = batched(roots_prev, factor)
    factor_sq = batched(factor, factor)
    moment = batched(batched(factor_sq, factor_sq), moment)
    factor = (5.0 * identity - moment) * 0.25
    roots_next = batched(iterate, factor)
    other_root = partner(roots_next, "fsdp", 0)
    left_root = jnp.where(is_left, roots_next, other_root)
    right_root = jnp.where(is_left, other_root, roots_next)
    left_rows = lax.dynamic_slice_in_dim(left_root, side_bit * half_rows, half_rows, 1)
    own_part = batched(batched(left_rows, grad_block), right_root)
    own_energy = jnp.sum(own_part * own_part, axis=(1, 2))
    energy = own_energy + partner(own_energy, "fsdp", 0)
    norm_value = jnp.sqrt(energy / (block_size * block_size) + NORM_EPSILON)
    update = (own_part / norm_value[:, None, None]).astype(jnp.bfloat16)
    replica = lax.axis_index("dp")
    col_width = kv_width // replica_count
    col_first = replica * col_width
    col_block = col_first // block_size
    col_offset = col_first % block_size
    outgoing = lax.dynamic_slice_in_dim(update, col_offset, col_width, 2)
    incoming = lax.all_gather(outgoing, "fsdp", axis=0, tiled=True)
    shard_height = weight.shape[0]
    piece_rows = min(shard_height, half_rows)
    col_blocks = kv_width // block_size
    positions = jnp.arange(owner_table.shape[0], dtype=jnp.int32)
    device = lax.axis_index("fsdp")
    row_first = device * shard_height + 0
    block_row = row_first // block_size
    half_bit = row_first % block_size // half_rows
    row_offset = row_first % half_rows
    wanted = block_row * col_blocks + col_block
    location = jnp.sum(jnp.where(owner_table == wanted, positions, 0))
    holder = location // slot_count * 2 + half_bit
    table_entry = holder * slot_count + location % slot_count
    span = lax.dynamic_slice(
        incoming, (table_entry, row_offset, jnp.int32(0)), (1, piece_rows, col_width)
    )
    pieces = [span[0]]
    direction = jnp.concatenate(pieces, axis=0)
    return (projected, input_grad, roots_next, direction)


def solution(mesh):
    placed = (
        P(("dp", "fsdp"), None),
        P(("dp", "fsdp"), None),
        P("fsdp", None),
        P(),
        P("fsdp", None, None),
        P("fsdp", None, None),
    )
    return jax.shard_map(
        local,
        mesh=mesh,
        in_specs=placed,
        out_specs=(
            P(("dp", "fsdp"), None),
            P(("dp", "fsdp"), None),
            P("fsdp", None, None),
            P("fsdp", "dp"),
        ),
        check_vma=False,
    )
```

profile of v0, /device:TPU:8, one launch (start us, length us, event | category | flops | bytes accessed | tf_op | source)
XLA Modules:
  0.0 765.2 jit_solution(11622585521024637621)
XLA Ops:
  7.2 233.2 %while.13 = (s32[]{:T(128)}, f32[32,256,512]{2,1,0:T(8,128)}, s32[32]{0:T(128)S(1)}, s32[16]{0:T(128)}, bf16[128,4096]{1,0:T(8,128)(2,1)}, /*index=5*/bf16[128,1...) while((s32[]{:T(128)}, f32[32,256,512]{2,1,0:T(8,128)}, ...), condition=%wide.region_1.2_spmd, body=%wide.region_0.1_spmd.sunk | while | flops 33554524 | bytes 722539 | solution.py:77
  12.5 2.1 fusion.67
  19.7 2.1 fusion.67
  23.1 1.2 dynamic_slice.64
  27.0 2.1 fusion.67
  34.3 2.1 fusion.67
  41.6 2.1 fusion.67
  48.9 2.1 fusion.67
  56.1 2.1 fusion.67
  63.4 2.1 fusion.67
  70.7 2.1 fusion.67
  74.1 1.2 dynamic_slice.64
  78.0 2.1 fusion.67
  85.2 2.1 fusion.67
  92.6 2.1 fusion.67
  96.0 1.2 dynamic_slice.64
  99.8 2.1 fusion.67
  107.1 2.1 fusion.67
  114.4 2.1 fusion.67
  117.8 1.2 dynamic_slice.64
  121.7 2.2 fusion.67
  129.0 2.1 fusion.67
  136.3 2.1 fusion.67
  139.8 1.2 dynamic_slice.64
  143.7 2.1 fusion.67
  150.9 2.1 fusion.67
  158.2 2.1 fusion.67
  165.5 2.1 fusion.67
  172.8 2.1 fusion.67
  180.1 2.1 fusion.67
  187.4 2.1 fusion.67
  194.6 2.1 fusion.67
  198.1 1.2 dynamic_slice.64
  202.0 2.1 fusion.67
  209.2 2.1 fusion.67
  216.5 2.1 fusion.67
  223.8 2.1 fusion.67
  231.1 2.1 fusion.67
  238.4 2.1 fusion.67
  240.5 17.4 %copy.12 = f32[8192,512]{0,1:T(8,128)} copy(f32[8192,512]{1,0:T(8,128)} %bitcast.70) | data formatting | bytes 33554432 | tf_op jit(solution)/shard_map/reshape | solution.py:81
  258.0 249.2 %reduce-scatter.2.cloned.1.call-done = f32[256,512]{0,1:T(8,128)} async-done(((f32[8192,512]{0,1:T(8,128)}), f32[256,512]{0,1:T(8,128)}) %reduce-scatter.2.cloned.1.call-update) | async-done | bytes 524304 | tf_op jit(solution)/shard_map/reduce_scatter | solution.py:80
  508.0 63.6 %all-reduce.2.cloned.1.call-done = f32[1,256,512]{1,2,0:T(8,128)} async-done(((f32[1,256,512]{1,2,0:T(8,128)}), f32[1,256,512]{1,2,0:T(8,128)}) %all-reduce.2.cloned.1.call-update) | async-done | bytes 524304 | tf_op jit(solution)/shard_map/psum | solution.py:86
  571.6 1.6 collective-permute-start
  573.1 1.8 fusion.17
  575.0 2.8 fusion.46
  577.8 5.6 collective-permute-done
  585.7 1.6 copy.11
  587.2 4.8 select_reduce_fusion
  592.6 3.4 fusion.12
  596.1 1.9 fusion.21
  598.0 3.5 fusion.15
  601.5 2.0 fusion.47
  603.6 1.9 fusion.5
  605.4 1.8 convolution_bitcast_fusion.1
  607.3 1.5 collective-permute-start.1
  608.8 31.0 %collective-permute-done.1 = f32[1,512,512]{2,1,0:T(8,128)} collective-permute-done((f32[1,512,512]{2,1,0:T(8,128)S(1)}, f32[1,512,512]{2,1,0:T(8,128)}, u32[]{:S(2)}, u32[]{:S(2)}) %collective-permute-start.1) | collective-permute-done | bytes 1048608 | tf_op jit(solution)/shard_map/ppermute | solution.py:12
  639.8 2.1 fusion.10
  642.0 3.2 multiply_reduce_fusion
  645.9 2.8 collective-permute-done.2
  652.1 22.1 %all-gather.4.cloned.1.call-done = bf16[4096,1024]{1,0:T(8,128)(2,1)} async-done(((bf16[128,1024]{1,0:T(8,128)(2,1)}), bf16[4096,1024]{1,0:T(8,128)(2,1)}) %all-gather.4.cloned.1.call-update) | async-done | bytes 8388624 | tf_op jit(solution)/shard_map/all_gather | solution.py:51
  674.3 7.4 convolution_convert_fusion
  681.7 2.0 convolution_convert_fusion.1
  683.6 73.6 %all-gather.6.cloned.1.call-done = bf16[8192,128]{1,0:T(8,128)(2,1)} async-done(((bf16[256,128]{1,0:T(8,128)(2,1)}), bf16[8192,128]{1,0:T(8,128)(2,1)}) %all-gather.6.cloned.1.call-update) | async-done | bytes 2097168 | tf_op jit(solution)/shard_map/all_gather | solution.py:123
  757.3 1.4 dynamic-slice_bitcast_fusion
  (85 shorter events, 56.2 us)
Async XLA Ops:
  7.2 566.0 %copy-start = (f32[1,512,512]{2,1,0:T(8,128)S(1)}, f32[1,512,512]{2,1,0:T(8,128)}, u32[]{:S(2)}) copy-start(f32[1,512,512]{2,1,0:T(8,128)} %param.13) | copy-start | bytes 3145732
  7.2 500.0 %reduce-scatter.2.cloned.1.call-start = ((), (), s32[]{:S(2)}) async-start(), calls=%async_computation.2 | async-start | bytes 17301504 | tf_op jit(solution)/shard_map/reduce_scatter | solution.py:80
  257.9 313.6 %all-reduce.2.cloned.1.call-start = ((), (), s32[]{:S(2)}) async-start(), calls=%async_computation.3 | async-start | bytes 1048576 | tf_op jit(solution)/shard_map/psum | solution.py:86
  507.2 167.1 %all-gather.4.cloned.1.call-start = ((), (), s32[]{:S(2)}) async-start(), calls=%async_computation.1 | async-start | bytes 8650752 | tf_op jit(solution)/shard_map/all_gather | solution.py:51
  507.9 249.3 %all-gather.6.cloned.1.call-start = ((), (), s32[]{:S(2)}) async-start(), calls=%async_computation.4 | async-start | bytes 2162688 | tf_op jit(solution)/shard_map/all_gather | solution.py:123
  571.6 11.8 %collective-permute-start = (f32[1,256,512]{1,2,0:T(8,128)}, f32[1,256,512]{1,2,0:T(8,128)S(1)}, u32[]{:S(2)}, u32[]{:S(2)}) collective-permute-start(f32[1,256,512]{1,2,0:T(8,128)} %all-reduce.2.cloned.1.call-done), channel_id=1, source_target_pairs={{0,1},{1,0},{2,3},{3,2},{4,5},{5,4},{6,7},{7,6},{8,9},{9,8},{10,11... | collective-permute-start | bytes 1572872 | tf_op jit(solution)/shard_map/ppermute | solution.py:12
  601.5 49.3 %copy-start.5 = (s32[16]{0:T(128)S(1)}, s32[16]{0:T(128)}, u32[]{:S(2)}) copy-start(s32[16]{0:T(128)} %get-tuple-element.250) | copy-start | bytes 196
  601.5 72.8 %copy-start.4 = (bf16[128,1024]{1,0:T(8,128)(2,1)S(1)}, bf16[128,1024]{1,0:T(8,128)(2,1)}, u32[]{:S(2)}) copy-start(bf16[128,1024]{1,0:T(8,128)(2,1)} %get-tuple-element.238) | copy-start | bytes 786436
  607.3 76.4 %copy-start.2 = (f32[1,512,512]{2,1,0:T(8,128)}, f32[1,512,512]{2,1,0:T(8,128)S(1)}, u32[]{:S(2)}) copy-start(f32[1,512,512]{2,1,0:T(8,128)S(1)} %convolution_bitcast_fusion.1) | copy-start | bytes 3145732
  607.3 32.5 %collective-permute-start.1 = (f32[1,512,512]{2,1,0:T(8,128)S(1)}, f32[1,512,512]{2,1,0:T(8,128)}, u32[]{:S(2)}, u32[]{:S(2)}) collective-permute-start(f32[1,512,512]{2,1,0:T(8,128)S(1)} %convolution_bitcast_fusion.1), channel_id=1, source_target_pairs={{0,1},{1,0},{2,3},{3,2},{4,5},{5,4},{6,7},{7,6},{8,9},{9,8},{10,11... | collective-permute-start | bytes 3145736 | tf_op jit(solution)/shard_map/ppermute | solution.py:12
  642.0 39.7 %copy-start.3 = (bf16[128,4096]{1,0:T(8,128)(2,1)S(1)}, bf16[128,4096]{1,0:T(8,128)(2,1)}, u32[]{:S(2)}) copy-start(bf16[128,4096]{1,0:T(8,128)(2,1)} %get-tuple-element.237) | copy-start | bytes 3145732
  645.1 3.6 collective-permute-start.2
  674.3 7.4 copy-start.1
Sparse Core Ops, SparseCore 0:
  258.1 249.0 reduce-scatter.1
  509.5 62.0 all-reduce.1
  574.5 99.6 all-gather.3
  677.0 80.1 all-gather.5
where the time goes:
time: 768 us; the launch traced here: 765 us
  waiting for transfers between devices  449 us (58%)
  loops' own time  108 us (14%)
  matrix products  106 us (14%)
  local copies, waits for them, and re-layouts  78.8 us (10%)
  between operations  16.6 us (2%)
    reduce_scatter x1, waiting for transfers between devices, local(): lax.psum_scatter(term_rows.reshape(own_rows * lax.axis_size('fsdp'), bloc...  249 us
    another operation x1, loops' own time, local(): lax.map(unit_term, jnp.arange(own_rows * lax.axis_size('fsdp') // half_ro...  108 us
    all_gather x1, waiting for transfers between devices, local(): incoming = lax.all_gather(outgoing, 'fsdp', axis=0, tiled=True)  73.6 us
    dot_general x32, matrix products, grad_rows(): lax.dot_general(token_cols, upstream_cols, (((0,), (0,)), ((), ())), pref...  67.1 us
    psum x1, waiting for transfers between devices, local(): summed = lax.psum(partial_sum, 'dp')  63.6 us
    dynamic_slice x32, local copies, waits for them, and re-layouts, grad_rows(): lax.dynamic_index_in_dim(owner_table, table_entry, 0, keepdims=False)  39.7 us
    ppermute x3, waiting for transfers between devices, partner(): lax.ppermute(x, axis, [(i, i ^ 1 << stride) for i in range(lax.axis_size(...  39.4 us
    dot_general x11, matrix products, batched(): return jnp.einsum('sij,sjk->sik', left, right, precision=HIGHEST)  29.3 us
  transfers between devices with their start and end apart: 7, of which 7 were waited for; matrix products, arithmetic and copies ran while one was open for 6% of the time, Pallas kernels for 0%

commit v1 on v0

v1 whole, which is shorter than its diff:
```python
import functools

import jax
import jax.numpy as jnp
from jax import lax
from jax.experimental import pallas as pl
from jax.experimental.pallas import tpu as pltpu
from jax.sharding import PartitionSpec as P

HIGH = lax.Precision.HIGH
STAT_DECAY = 0.8
NORM_EPSILON = 1e-06
MESH = pl.DeviceIdType.MESH
VMEM_LIMIT = 48 * 1024 * 1024

NX, NY, NZ = 4, 4, 8
BS = 512
ROWS = 128
COLS = 256
HALF = 64
NB = 16


def remote(src, dst, send, recv, dp, fsdp):
    return pltpu.make_async_remote_copy(
        src_ref=src,
        dst_ref=dst,
        send_sem=send,
        recv_sem=recv,
        device_id=(dp, fsdp),
        device_id_type=MESH,
    )


def greet(peers):
    barrier = pltpu.get_barrier_semaphore()
    for dp, fsdp in peers:
        pl.semaphore_signal(barrier, inc=1, device_id=(dp, fsdp), device_id_type=MESH)
    pl.semaphore_wait(barrier, len(peers))


def lanes(start, size):
    return pl.ds(pl.multiple_of(start, 128), size)


def pool_kernel(tok, ups, tok_out, ups_out, t_send, t_recv, f_send, f_recv, u_send, u_recv, own):
    me, fs = lax.axis_index("dp"), lax.axis_index("fsdp")
    y, core = me // 2, me % 2
    sibling = y * 2 + 1 - core
    greet([(lax.rem(me + d, 8), fs) for d in range(1, 8)])

    def token_parts(to_y, where):
        for r in range(8):
            yield tok.at[:, lanes(512 * r + 128 * to_y, 128)], where.at[me, :, pl.ds(128 * r, 128)]

    def upstream_parts(to_core):
        for b in range(2):
            yield ups.at[:, lanes(512 * b + 256 * to_core, 256)], ups_out.at[b, me]

    for d in (1, 3, 2):
        to_y = lax.rem(y + d, 4)
        for src, dst in token_parts(to_y, tok_out):
            remote(src, dst, t_send.at[d], t_recv.at[d], to_y * 2 + core, fs).start()
    for src, dst in token_parts(y, tok_out):
        remote(src, dst, f_send.at[0], f_recv.at[0], sibling, fs).start()
    for d in (1, 3, 2, 0):
        to_y = lax.rem(y + d, 4)
        for flip in range(2):
            if d == 0 and flip == 0:
                continue
            to_core = core if flip == 0 else 1 - core
            for src, dst in upstream_parts(to_core):
                k = 2 * d + flip
                remote(src, dst, u_send.at[k], u_recv.at[k], to_y * 2 + to_core, fs).start()
    for src, dst in token_parts(y, tok_out):
        pltpu.make_async_copy(src, dst, own.at[0]).start()
    for src, dst in upstream_parts(core):
        pltpu.make_async_copy(src, dst, own.at[1]).start()

    def whole(send, recv, buf, slot):
        return remote(buf.at[slot], buf.at[slot], send, recv, sibling, fs)

    def both(send, recv, slot):
        return remote(ups_out.at[:, slot], ups_out.at[:, slot], send, recv, sibling, fs)

    for d in (1, 3, 2):
        slot = lax.rem(y + 4 - d, 4) * 2 + core
        whole(t_send.at[d], t_recv.at[d], tok_out, slot).wait_recv()
        whole(f_send.at[d], f_recv.at[d], tok_out, slot).start()
    for d in range(4):
        slot = lax.rem(y + 4 - d, 4) * 2 + 1 - core
        whole(f_send.at[d], f_recv.at[d], tok_out, slot).wait()
        if d:
            whole(t_send.at[d], t_recv.at[d], tok_out, slot).wait_send()
    for d in range(4):
        for flip in range(2):
            if d == 0 and flip == 0:
                continue
            from_core = core if flip == 0 else 1 - core
            slot = lax.rem(y + 4 - d, 4) * 2 + from_core
            k = 2 * d + flip
            both(u_send.at[k], u_recv.at[k], slot).wait()
    pltpu.make_async_copy(tok_out.at[me], tok_out.at[me], own.at[0]).wait()
    pltpu.make_async_copy(ups_out.at[:, me], ups_out.at[:, me], own.at[1]).wait()


def pool(tokens, upstream):
    rows = tokens.shape[0]
    dma = pltpu.SemaphoreType.DMA
    return pl.pallas_call(
        pool_kernel,
        out_shape=(
            jax.ShapeDtypeStruct((8, rows, 1024), jnp.bfloat16),
            jax.ShapeDtypeStruct((2, 8, rows, 256), jnp.bfloat16),
        ),
        in_specs=[pl.BlockSpec(memory_space=pl.ANY)] * 2,
        out_specs=(pl.BlockSpec(memory_space=pl.ANY),) * 2,
        scratch_shapes=[dma((4,)), dma((4,)), dma((4,)), dma((4,)), dma((8,)), dma((8,)), dma((2,))],
        compiler_params=pltpu.CompilerParams(
            collective_id=0, has_side_effects=True, vmem_limit_bytes=VMEM_LIMIT
        ),
        cost_estimate=pl.CostEstimate(flops=0, bytes_accessed=64 << 20, transcendentals=0),
    )(tokens, upstream)


def sum_kernel(
    table, part0, part1, block, outgoing, xbuf, xsum, zbuf, x_send, x_recv, z_send, z_recv, g_send, g_recv, f_send, f_recv
):
    me, fs = lax.axis_index("dp"), lax.axis_index("fsdp")
    y, core, x, z = me // 2, me % 2, fs // 8, fs % 8
    side = z % 2
    sibling = y * 2 + 1 - core
    mate = x * 8 + z + 1 - 2 * side

    peers = [(me, lax.rem(x + d, 4) * 8 + z) for d in range(1, 4)]
    peers += [(me, x * 8 + lax.rem(z + d, 8)) for d in range(1, 8)]
    peers += [(lax.rem(y + d, 4) * 2 + core, fs) for d in range(1, 4)]
    peers += [(lax.rem(y + d, 4) * 2 + core, mate) for d in range(1, 4)]
    peers += [(sibling, fs)]
    greet(peers)

    def arrange(x_to):
        def body(i, _):
            g = x_to * 4 + i
            chosen = table[g]
            band = lax.div(chosen, 2)
            piece = jnp.where(lax.rem(chosen, 2) == 0, part0[band], part1[band])
            outgoing[2 * g] = piece[:HALF]
            outgoing[2 * g + 1] = piece[HALF:]
            return 0

        lax.fori_loop(0, 4, body, 0)

    def x_copy(d):
        to = lax.rem(x + d, 4)
        return remote(
            outgoing.at[pl.ds(to * 8, 8)], xbuf.at[d], x_send.at[d], x_recv.at[d], me, to * 8 + z
        )

    for d in (2, 1, 3, 0):
        arrange(lax.rem(x + d, 4))
        if d:
            x_copy(d).start()
    for d in (1, 3, 2):
        x_copy(d).wait_recv()

    def z_copy(d):
        to = lax.rem(z + d, 8)
        return remote(xsum.at[to], zbuf.at[d], z_send.at[d], z_recv.at[d], me, x * 8 + to)

    for d in (4, 3, 5, 2, 6, 1, 7, 0):
        to = lax.rem(z + d, 8)
        xsum[to] = (outgoing[x * 8 + to] + xbuf[1, to]) + (xbuf[2, to] + xbuf[3, to])
        if d:
            z_copy(d).start()
    total = xsum[z]
    for d in (1, 7, 2, 6, 3, 5, 4):
        z_copy(d).wait_recv()
        total = total + zbuf[d]

    def place(of_y, of_side, of_core):
        return block.at[pl.ds(pl.multiple_of(of_y * ROWS + of_side * HALF, HALF), HALF), lanes(of_core * COLS, COLS)]

    own = place(y, side, core)
    own[...] = total

    def g_copy(d, flip, spot):
        fs_to = mate if flip else fs
        k = 2 * d + flip
        return remote(spot, spot, g_send.at[k], g_recv.at[k], lax.rem(y + d, 4) * 2 + core, fs_to)

    order = [(d, flip) for d in (2, 1, 3, 0) for flip in range(2) if d or flip]
    for d, flip in order:
        g_copy(d, flip, own).start()

    def f_copy(k, spot):
        return remote(spot, spot, f_send.at[k], f_recv.at[k], sibling, fs)

    f_copy(0, own).start()
    for d, flip in reversed(order):
        spot = place(lax.rem(y + 4 - d, 4), 1 - side if flip else side, core)
        g_copy(d, flip, spot).wait_recv()
        f_copy(2 * d + flip, spot).start()
    for d in range(4):
        for flip in range(2):
            spot = place(lax.rem(y + 4 - d, 4), 1 - side if flip else side, 1 - core)
            f_copy(2 * d + flip, spot).wait()
    for d in (1, 2, 3):
        x_copy(d).wait_send()
    for d in range(1, 8):
        z_copy(d).wait_send()
    for d, flip in order:
        g_copy(d, flip, own).wait_send()


def sum_blocks(table, parts):
    dma = pltpu.SemaphoreType.DMA
    f32 = jnp.float32
    return pl.pallas_call(
        sum_kernel,
        out_shape=jax.ShapeDtypeStruct((BS, BS), f32),
        in_specs=[pl.BlockSpec(memory_space=pltpu.SMEM)] + [pl.BlockSpec(memory_space=pltpu.VMEM)] * 2,
        out_specs=pl.BlockSpec(memory_space=pltpu.VMEM),
        scratch_shapes=[
            pltpu.VMEM((32, HALF, COLS), f32),
            pltpu.VMEM((4, 8, HALF, COLS), f32),
            pltpu.VMEM((8, HALF, COLS), f32),
            pltpu.VMEM((8, HALF, COLS), f32),
        ]
        + [dma((4,)), dma((4,))]
        + [dma((8,))] * 6,
        compiler_params=pltpu.CompilerParams(
            collective_id=1, has_side_effects=True, vmem_limit_bytes=VMEM_LIMIT
        ),
        cost_estimate=pl.CostEstimate(flops=0, bytes_accessed=64 << 20, transcendentals=0),
    )(table, *parts)


def finish_kernel(
    inverse, left_rows, root, out, rows_in, energies, chunks, spread, picked,
    a_send, a_recv, e_send, e_recv, s_send, s_recv, p_send, p_recv, local
):
    me, fs = lax.axis_index("dp"), lax.axis_index("fsdp")
    z = fs % 8
    group, side = fs // 2, z % 2
    piece = z % 4
    sources = [(2 * piece + i, 2 * (4 * q + me % 4) + 1, i, q) for i in range(2) for q in range(4)]
    my_piece, my_quarter, my_cols = me // 2, group // 4, group % 4
    places = [
        (4 * cb + my_cols, 4 * rb + my_piece, 2 * rb + cb) for rb in range(8) for cb in range(2)
    ]
    barrier = pltpu.get_barrier_semaphore()

    def tell(dp, fsdp):
        pl.semaphore_signal(barrier, inc=1, device_id=(dp, fsdp), device_id_type=MESH)

    for dp, fsdp, _, _ in sources:
        @pl.when(jnp.logical_or(dp != me, fsdp != fs))
        def _(dp=dp, fsdp=fsdp):
            tell(dp, fsdp)

    def out_rows(i, q):
        return out.at[pl.ds(pl.multiple_of(HALF * i + 16 * q, 16), 16)]

    def a_copy():
        return remote(left_rows, rows_in, a_send, a_recv, me, fs + 1 - 2 * side)

    @pl.when(side == 0)
    def _():
        pl.semaphore_wait(barrier, 1)
        a_copy().start()
        a_copy().wait_send()

    @pl.when(side == 1)
    def _():
        tell(me, fs - 1)
        for d in range(1, 8):
            tell(lax.rem(me + d, 8), fs)
        for d in range(1, NB):
            tell(me, lax.rem(fs + 2 * d, 32))
        is_own = jnp.int32(0)
        for dp, fsdp, _ in places:
            is_own += jnp.where(jnp.logical_and(dp == me, fsdp == fs), 1, 0)
        pl.semaphore_wait(barrier, 7 + 15 + 16 - is_own)

        a_copy().wait_recv()
        product = jnp.dot(
            rows_in[...], root[...], precision=lax.Precision.HIGHEST, preferred_element_type=jnp.float32
        )
        energy = jnp.sum(product * product)
        energies[0] = jnp.full((8, 128), energy, jnp.float32)

        def e_copy(d):
            return remote(
                energies.at[0], energies.at[d], e_send.at[d], e_recv.at[d], lax.rem(me + d, 8), fs
            )

        for d in range(1, 8):
            e_copy(d).start()
        for d in range(1, 8):
            e_copy(d).wait_recv()

        total = jnp.zeros((8, 128), jnp.float32)
        for dp in range(8):
            total = total + energies[lax.rem(me - dp + 8, 8)]
        mean = total[0:1, 0:1] / (BS * BS)
        update = (product / jnp.sqrt(mean + NORM_EPSILON)).astype(jnp.bfloat16)
        for j in range(NB):
            q, k = j // 4, j % 4
            chunks[j] = update[16 * q : 16 * q + 16, 128 * k : 128 * k + 128]

        def s_copy(d):
            to = lax.rem(group + d, NB)
            return remote(
                chunks.at[to], spread.at[group], s_send.at[d], s_recv.at[d], me, 2 * to + 1
            )

        for d in range(1, NB):
            s_copy(d).start()
        spread[group] = chunks[group]
        for d in range(1, NB):
            source = lax.rem(group + NB - d, NB)
            remote(
                chunks.at[0], spread.at[source], s_send.at[d], s_recv.at[d], me, 2 * source + 1
            ).wait_recv()
        for dp, fsdp, b in places:
            picked[b] = spread[inverse[b]]

        def p_copy(dp, fsdp, b):
            i, q = me % 2, my_quarter
            return remote(picked.at[b], out_rows(i, q), p_send.at[b], p_recv.at[4 * i + q], dp, fsdp)

        for dp, fsdp, b in places:
            mine = jnp.logical_and(dp == me, fsdp == fs)

            @pl.when(mine)
            def _(b=b):
                copy = pltpu.make_async_copy(picked.at[b], out_rows(me % 2, my_quarter), local)
                copy.start()
                copy.wait()

            @pl.when(jnp.logical_not(mine))
            def _(dp=dp, fsdp=fsdp, b=b):
                p_copy(dp, fsdp, b).start()

        for d in range(1, 8):
            e_copy(d).wait_send()
        for d in range(1, NB):
            s_copy(d).wait_send()
        for dp, fsdp, b in places:
            @pl.when(jnp.logical_or(dp != me, fsdp != fs))
            def _(dp=dp, fsdp=fsdp, b=b):
                p_copy(dp, fsdp, b).wait_send()

    for dp, fsdp, i, q in sources:
        @pl.when(jnp.logical_or(dp != me, fsdp != fs))
        def _(dp=dp, fsdp=fsdp, i=i, q=q):
            remote(picked.at[0], out_rows(i, q), p_send.at[0], p_recv.at[4 * i + q], dp, fsdp).wait_recv()


def finish(inverse, left_rows, root):
    dma = pltpu.SemaphoreType.DMA
    f32, b16 = jnp.float32, jnp.bfloat16
    vmem = pl.BlockSpec(memory_space=pltpu.VMEM)
    return pl.pallas_call(
        finish_kernel,
        out_shape=jax.ShapeDtypeStruct((128, 128), b16),
        in_specs=[pl.BlockSpec(memory_space=pltpu.SMEM), vmem, vmem],
        out_specs=vmem,
        scratch_shapes=[
            pltpu.VMEM((HALF, BS), f32),
            pltpu.VMEM((8, 8, 128), f32),
            pltpu.VMEM((NB, 16, 128), b16),
            pltpu.VMEM((NB, 16, 128), b16),
            pltpu.VMEM((NB, 16, 128), b16),
            dma(()),
            dma(()),
            dma((8,)),
            dma((8,)),
            dma((NB,)),
            dma((NB,)),
            dma((NB,)),
            dma((8,)),
            dma(()),
        ],
        compiler_params=pltpu.CompilerParams(
            collective_id=2, has_side_effects=True, vmem_limit_bytes=VMEM_LIMIT
        ),
        cost_estimate=pl.CostEstimate(flops=0, bytes_accessed=32 << 20, transcendentals=0),
    )(inverse, left_rows, root)


def mm(left, right):
    return jnp.dot(left, right, precision=HIGH, preferred_element_type=jnp.float32)


def newton(grad_block, stats_prev, root_prev, is_left):
    chosen = jnp.where(is_left, grad_block, grad_block.T)
    gram = mm(chosen, chosen.T)
    stats = STAT_DECAY * stats_prev + (1.0 - STAT_DECAY) * gram
    normed = stats / (jnp.trace(stats) / BS)
    identity = jnp.eye(BS, dtype=jnp.float32)
    square = mm(root_prev, root_prev)
    moment = mm(mm(square, square), normed)
    factor = (5.0 * identity - moment) * 0.25
    iterate = mm(root_prev, factor)
    factor_sq = mm(factor, factor)
    moment = mm(mm(factor_sq, factor_sq), moment)
    factor = (5.0 * identity - moment) * 0.25
    return mm(iterate, factor)


def local(tokens, upstream, weight, owner_table, stats_prev, roots_prev):
    dp, fs = lax.axis_index("dp"), lax.axis_index("fsdp")
    full_weight = lax.all_gather(weight, "fsdp", axis=0, tiled=True)

    tok_pool, ups_pool = pool(tokens, upstream)
    parts = [
        lax.dot_general(
            tok_pool.reshape(-1, 1024),
            ups_pool[b].reshape(-1, COLS),
            (((0,), (0,)), ((), ())),
            preferred_element_type=jnp.float32,
        ).reshape(8, ROWS, COLS)
        for b in range(2)
    ]
    grad_block = sum_blocks(owner_table, parts)
    is_left = fs % 2 == 0
    root = newton(grad_block, stats_prev[0], roots_prev[0], is_left)
    left_rows = mm(lax.dynamic_slice_in_dim(root, dp * HALF, HALF, 0), grad_block)
    positions = jnp.arange(NB, dtype=jnp.int32)
    inverse = jnp.sum(
        jnp.where(owner_table[None, :] == positions[:, None], positions[None, :], 0), axis=1
    )
    direction = finish(inverse, left_rows, root)

    tokens, upstream, direction = lax.optimization_barrier((tokens, upstream, direction))
    projected = jnp.dot(tokens, full_weight, preferred_element_type=jnp.float32).astype(jnp.bfloat16)
    input_grad = lax.dot_general(
        upstream, full_weight, (((1,), (1,)), ((), ())), preferred_element_type=jnp.float32
    ).astype(jnp.bfloat16)
    return projected, input_grad, root[None], direction


def solution(mesh):
    placed = (
        P(("dp", "fsdp"), None),
        P(("dp", "fsdp"), None),
        P("fsdp", None),
        P(),
        P("fsdp", None, None),
        P("fsdp", None, None),
    )
    return jax.shard_map(
        local,
        mesh=mesh,
        in_specs=placed,
        out_specs=(
            P(("dp", "fsdp"), None),
            P(("dp", "fsdp"), None),
            P("fsdp", None, None),
            P("fsdp", "dp"),
        ),
        check_vma=False,
    )
```

time: 768 us -> 178 us (0.23)
  waiting for transfers between devices: 449 us -> 0.7 us
  Pallas kernels: 0 us -> 129 us
  loops' own time: 108 us -> 0 us
  matrix products: 106 us -> 24.3 us
  local copies, waits for them, and re-layouts: 78.8 us -> 8.8 us
    reduce_scatter x1 -> x0, waiting for transfers between devices: 249 us -> none  [local(): lax.psum_scatter(term_rows.reshape(own_rows * lax.axis_size('fsdp'), bloc...]
    pallas_call x0 -> x3, Pallas kernels: none -> 129 us  [the longest x1 77.4 us: sum_blocks(): pl.pallas_call(sum_kernel, out_shape=jax.ShapeDtypeStruct((BS, BS), f32),...]
    another operation x1 -> x0, loops' own time: 108 us -> none  [local(): lax.map(unit_term, jnp.arange(own_rows * lax.axis_size('fsdp') // half_ro...]
    all_gather x2 -> x1, waiting for transfers between devices: 95.8 us -> 0.02 us  [local(): full_weight = lax.all_gather(weight, 'fsdp', axis=0, tiled=True)]
    dot_general x45 -> x14, matrix products: 106 us -> 24.3 us  [the longest x10 13.5 us: mm(): jnp.dot(left, right, precision=HIGH, preferred_element_type=jnp.float32)]
    psum x1 -> x0, waiting for transfers between devices: 63.6 us -> none  [local(): summed = lax.psum(partial_sum, 'dp')]
    dynamic_slice x64 -> x0, local copies, waits for them, and re-layouts: 58.4 us -> none  [the longest x32 39.7 us: grad_rows(): lax.dynamic_index_in_dim(owner_table, table_entry, 0, keepdims=False)]
    ppermute x3 -> x0, waiting for transfers between devices: 39.4 us -> none  [partner(): lax.ppermute(x, axis, [(i, i ^ 1 << stride) for i in range(lax.axis_size(...]
  transfers between devices with their start and end apart: 7 -> 1, of which waited for: 7 -> 0; matrix products, arithmetic and copies ran while one was open for 6% -> 11% of each run, Pallas kernels for 0% -> 73%
where the time goes in v1:
time: 178 us
  Pallas kernels  129 us (72%)
  matrix products  24.3 us (14%)
  between operations  14.9 us (8%)
  local copies, waits for them, and re-layouts  8.8 us (5%)
    pallas_call x1, Pallas kernels, sum_blocks(): pl.pallas_call(sum_kernel, out_shape=jax.ShapeDtypeStruct((BS, BS), f32),...  77.4 us
    pallas_call x1, Pallas kernels, pool(): pl.pallas_call(pool_kernel, out_shape=(jax.ShapeDtypeStruct((8, rows, 102...  27.6 us
    pallas_call x1, Pallas kernels, finish(): pl.pallas_call(finish_kernel, out_shape=jax.ShapeDtypeStruct((128, 128),...  24.3 us
    dot_general x10, matrix products, mm(): jnp.dot(left, right, precision=HIGH, preferred_element_type=jnp.float32)  13.5 us
    dot_general x1, matrix products, local(): lax.dot_general(upstream, full_weight, (((1,), (1,)), ((), ())), preferre...  7.39 us
    unnamed x23, local copies, waits for them, and re-layouts  4.42 us
  transfers between devices with their start and end apart: 1, of which 0 were waited for; matrix products, arithmetic and copies ran while one was open for 11% of the time, Pallas kernels for 73%

profile of v1, /device:TPU:8, one launch (start us, length us, event | category | flops | bytes accessed | tf_op | source)
XLA Modules:
  0.0 178.2 jit_solution(13127633524808267411)
XLA Ops:
  7.2 0.0 copy-start
  7.2 0.0 all-gather.2.cloned.1.call-start
  7.2 0.7 all-gather.2.cloned.1.call-update
  7.9 0.0 copy-start.1
  7.9 1.2 copy-done.1
  9.2 0.0 copy-start.4
  9.2 0.9 copy-done.4
  10.1 27.6 %shard_map.93 = (bf16[8,128,1024]{2,1,0:T(8,128)(2,1)S(1)}, bf16[2,8,128,256]{3,2,1,0:T(8,128)(2,1)S(1)}) custom-call(bf16[128,4096]{1,0:T(8,128)(2,1)S(1)} %copy-done.1, bf16[128,1024]{1,0:T(8,128)(2,1)S(1)} %copy-done.4), custom_call_target="tpu_custom_call" | custom-call | bytes 67108864 | tf_op jit(solution)/shard_map/pallas_call | solution.py:110
  37.7 0.0 copy-start.6
  37.7 1.0 copy-done.6
  38.7 2.6 %copy.12 = bf16[1024,1024]{1,0:T(8,128)(2,1)} copy(bf16[1024,1024]{0,1:T(8,128)(2,1)S(1)} %bitcast.42) | data formatting | bytes 4194304 | tf_op jit(solution)/shard_map/dot_general | solution.py:419
  41.3 0.0 copy-start.9
  41.3 1.4 fusion.29
  42.8 0.5 copy-done.9
  43.2 0.7 fusion.32.part1
  43.9 0.0 copy-start.7
  43.9 0.7 fusion.31.part0
  44.7 0.0 copy-done.7
  44.7 77.4 %shard_map.94 = f32[512,512]{1,0:T(8,128)S(1)} custom-call(s32[16]{0:T(128)S(1)} %copy-done.7, f32[8,128,256]{2,1,0:T(8,128)S(1)} %fusion.31.part0, f32[8,128,256]{2,1,0:T(8,128)S(1)} %fusion.32.part1), custom_call_target="tpu_custom_call" | custom-call | bytes 67108864 | tf_op jit(solution)/shard_map/pallas_call | solution.py:219
  122.1 0.3 copy.13
  122.5 3.9 %select_reduce_fusion = (f32[]{:T(128)}, f32[512,512]{1,0:T(8,128)}) fusion(f32[512,512]{1,0:T(8,128)S(1)} %shard_map.94, f32[512,512]{0,1:T(8,128)S(1)} %copy.13, pred[]{:T(512)S(6)} %eq.31, f32[1,512,512]{2,1,0:T(8,128)} %param.10), kind=kOutput, calls=%fused_computation.15 | convolution fusion | flops 807141376 | bytes 4194309 | tf_op jit(solution)/shard_map/dot_general | solution.py:394
  127.1 0.1 select_reduce_fusion.1.inverse
  127.2 0.0 copy-done
  127.2 1.0 fusion.5
  128.2 0.0 copy-start.10
  128.2 1.0 fusion.30
  129.3 0.2 copy-done.10
  129.4 1.0 fusion.7
  130.5 1.1 fusion.9
  131.5 1.9 %fusion.3 = f32[512,512]{1,0:T(8,128)S(1)} fusion(f32[1,512,512]{2,1,0:T(8,128)S(1)} %copy-done, f32[512,512]{1,0:T(8,128)S(1)} %fusion.7), kind=kOutput, calls=%fused_computation.9 | convolution fusion | flops 806354944 | bytes 3145728 | tf_op jit(solution)/shard_map/dot_general | solution.py:394
  133.4 1.0 fusion.33
  134.5 1.1 fusion.1
  135.5 0.0 copy-start.5
  135.5 1.1 fusion.34.root
  136.6 0.0 copy-start.3
  136.6 0.4 fusion.20.left_rows
  137.0 24.3 %shard_map.95 = bf16[128,128]{1,0:T(8,128)(2,1)S(1)} custom-call(s32[16]{0:T(128)S(1)} %select_reduce_fusion.1.inverse, f32[64,512]{1,0:T(8,128)S(1)} %fusion.20.left_rows, f32[512,512]{1,0:T(8,128)S(1)} %fusion.34.root), custom_call_target="tpu_custom_call" | custom-call | bytes 33554432 | tf_op jit(solution)/shard_map/pallas_call | solution.py:365
  161.3 0.0 copy-start.2
  161.3 0.0 all-gather.2.cloned.1.call-done
  161.4 0.0 copy-done.5
  161.4 0.0 copy-start.8
  161.4 7.4 %convolution_convert_fusion = bf16[128,4096]{1,0:T(8,128)(2,1)} fusion(bf16[128,1024]{1,0:T(8,128)(2,1)S(1)} %copy-done.5, bf16[4096,1024]{1,0:T(8,128)(2,1)} %all-gather.2.cloned.1.call-done), kind=kOutput, calls=%fused_computation | convolution fusion | flops 1074266112 | bytes 9699328 | tf_op jit(solution)/shard_map/dot_general | solution.py:439
  168.8 0.0 copy-done.3
  168.8 0.0 copy-done.2
  168.8 0.0 copy-done.8
  168.8 2.0 %convolution_convert_fusion.1 = bf16[128,1024]{1,0:T(8,128)(2,1)} fusion(bf16[128,4096]{1,0:T(8,128)(2,1)S(1)} %copy-done.2, bf16[4096,1024]{1,0:T(8,128)(2,1)S(1)} %copy-done.8), kind=kOutput, calls=%fused_computation.6 | convolution fusion | flops 1073872896 | bytes 9699328 | tf_op jit(solution)/shard_map/dot_general | solution.py:438
  170.8 0.6 copy.15
Async XLA Ops:
  7.2 120.0 %copy-start = (f32[1,512,512]{2,1,0:T(8,128)S(1)}, f32[1,512,512]{2,1,0:T(8,128)}, u32[]{:S(2)}) copy-start(f32[1,512,512]{2,1,0:T(8,128)} %param.11) | copy-start | bytes 3145732
  7.2 154.2 %all-gather.2.cloned.1.call-start = ((), (), s32[]{:S(2)}) async-start(), calls=%async_computation | async-start | bytes 8650752 | tf_op jit(solution)/shard_map/all_gather | solution.py:415
  7.9 1.2 copy-start.1
  9.2 0.9 copy-start.4
  37.7 1.0 copy-start.6
  41.3 1.9 %copy-start.9 = (bf16[1024,1024]{1,0:T(8,128)(2,1)S(1)}, bf16[1024,1024]{1,0:T(8,128)(2,1)}, u32[]{:S(2)}) copy-start(bf16[1024,1024]{1,0:T(8,128)(2,1)} %copy.12) | copy-start | bytes 6291460
  43.9 0.7 copy-start.7
  128.2 1.2 copy-start.10
  135.5 25.9 %copy-start.5 = (bf16[128,1024]{1,0:T(8,128)(2,1)S(1)}, bf16[128,1024]{1,0:T(8,128)(2,1)}, u32[]{:S(2)}) copy-start(bf16[128,1024]{1,0:T(8,128)(2,1)} %ups.1) | copy-start | bytes 786436
  136.6 32.2 %copy-start.3 = (f32[512,512]{1,0:T(8,128)}, f32[512,512]{1,0:T(8,128)S(1)}, u32[]{:S(2)}) copy-start(f32[512,512]{1,0:T(8,128)S(1)} %fusion.34.root) | copy-start | bytes 3145732
  161.3 7.5 %copy-start.2 = (bf16[128,4096]{1,0:T(8,128)(2,1)S(1)}, bf16[128,4096]{1,0:T(8,128)(2,1)}, u32[]{:S(2)}) copy-start(bf16[128,4096]{1,0:T(8,128)(2,1)} %tok.1) | copy-start | bytes 3145732
  161.4 7.4 %copy-start.8 = (bf16[4096,1024]{1,0:T(8,128)(2,1)S(1)}, bf16[4096,1024]{1,0:T(8,128)(2,1)}, u32[]{:S(2)}) copy-start(bf16[4096,1024]{1,0:T(8,128)(2,1)} %all-gather.2.cloned.1.call-done) | copy-start | bytes 25165828
Sparse Core Ops, SparseCore 0:
  10.6 125.4 all-gather.1

commit v2 on v1

--- a/solution.py
+++ b/solution.py
@@ -19,6 +19,8 @@
 COLS = 256
 HALF = 64
 NB = 16
+RA = 48
+WA = 768
 
 
 def remote(src, dst, send, recv, dp, fsdp):
@@ -43,197 +45,345 @@
     return pl.ds(pl.multiple_of(start, 128), size)
 
 
-def pool_kernel(tok, ups, tok_out, ups_out, t_send, t_recv, f_send, f_recv, u_send, u_recv, own):
+def gradient_kernel(
+    table, tok, ups, shard, block, weight,
+    tok_in, tok_t, ups_in, part, outgoing, xa_in, za_sum, za_in, zb_in, xb_sum, xb_in,
+    t_send, t_recv, f_send, f_recv, u_send, u_recv,
+    xa_send, xa_recv, za_send, za_recv, zb_send, zb_recv, xb_send, xb_recv,
+    g_send, g_recv, h_send, h_recv,
+    wza_send, wza_recv, wxa_send, wxa_recv, wzb_send, wzb_recv, wxb_send, wxb_recv,
+    wy_send, wy_recv, wc_send, wc_recv, own,
+):
     me, fs = lax.axis_index("dp"), lax.axis_index("fsdp")
-    y, core = me // 2, me % 2
+    y, core, x, z = me // 2, me % 2, fs // 8, fs % 8
+    side = z % 2
     sibling = y * 2 + 1 - core
-    greet([(lax.rem(me + d, 8), fs) for d in range(1, 8)])
-
-    def token_parts(to_y, where):
+    mate = x * 8 + z + 1 - 2 * side
+
+    def to_x(d):
+        return lax.rem(x + d, 4)
+
+    def to_y(d):
+        return lax.rem(y + d, 4)
+
+    def to_z(d):
+        return lax.rem(z + d, 8)
+
+    peers = [(lax.rem(me + d, 8), fs) for d in range(1, 8)]
+    peers += [(me, to_x(d) * 8 + z) for d in range(1, 4)]
+    peers += [(me, x * 8 + to_z(d)) for d in range(1, 8)]
+    peers += [(to_y(d) * 2 + core, mate) for d in range(1, 4)]
+    greet(peers)
+
+    def token_parts(of_y, where):
         for r in range(8):
-            yield tok.at[:, lanes(512 * r + 128 * to_y, 128)], where.at[me, :, pl.ds(128 * r, 128)]
-
-    def upstream_parts(to_core):
+            yield tok.at[:, lanes(512 * r + 128 * of_y, 128)], where.at[me, :, pl.ds(128 * r, 128)]
+
+    def upstream_parts(of_core):
         for b in range(2):
-            yield ups.at[:, lanes(512 * b + 256 * to_core, 256)], ups_out.at[b, me]
-
-    for d in (1, 3, 2):
-        to_y = lax.rem(y + d, 4)
-        for src, dst in token_parts(to_y, tok_out):
-            remote(src, dst, t_send.at[d], t_recv.at[d], to_y * 2 + core, fs).start()
-    for src, dst in token_parts(y, tok_out):
+            yield ups.at[:, lanes(512 * b + 256 * of_core, 256)], ups_in.at[b, me]
+
+    for d in (2, 1, 3):
+        for src, dst in token_parts(to_y(d), tok_in):
+            remote(src, dst, t_send.at[d], t_recv.at[d], to_y(d) * 2 + core, fs).start()
+    for src, dst in token_parts(y, tok_in):
         remote(src, dst, f_send.at[0], f_recv.at[0], sibling, fs).start()
-    for d in (1, 3, 2, 0):
-        to_y = lax.rem(y + d, 4)
+
+    own_rows = pl.ds(pl.multiple_of(64 * (y % 2) + 32 * core, 32), 32)
+    other_rows = pl.ds(pl.multiple_of(64 * (1 - y % 2) + 32 * core, 32), 32)
+    ca, cb = pl.ds(0, WA), pl.ds(WA, 1024 - WA)
+
+    def wza(d):
+        return remote(
+            shard.at[own_rows, ca], weight.at[x, z, own_rows, ca],
+            wza_send.at[d], wza_recv.at[d], me, x * 8 + to_z(d),
+        )
+
+    def wxb(d):
+        return remote(
+            shard.at[own_rows, cb], weight.at[x, z, own_rows, cb],
+            wxb_send.at[d], wxb_recv.at[d], me, to_x(d) * 8 + z,
+        )
+
+    def wxa(d):
+        slab = weight.at[x, :, own_rows, ca]
+        return remote(slab, slab, wxa_send.at[d], wxa_recv.at[d], me, to_x(d) * 8 + z)
+
+    def wzb(d):
+        slab = weight.at[:, z, own_rows, cb]
+        return remote(slab, slab, wzb_send.at[d], wzb_recv.at[d], me, x * 8 + to_z(d))
+
+    def wza_in(d):
+        spot = weight.at[x, lax.rem(z + 8 - d, 8), own_rows, ca]
+        return remote(spot, spot, wza_send.at[d], wza_recv.at[d], me, mate)
+
+    def wxb_in(d):
+        spot = weight.at[lax.rem(x + 4 - d, 4), z, own_rows, cb]
+        return remote(spot, spot, wxb_send.at[d], wxb_recv.at[d], me, mate)
+
+    def wxa_in(d):
+        spot = weight.at[lax.rem(x + 4 - d, 4), :, own_rows, ca]
+        return remote(spot, spot, wxa_send.at[d], wxa_recv.at[d], me, mate)
+
+    def wzb_in(d):
+        spot = weight.at[:, lax.rem(z + 8 - d, 8), own_rows, cb]
+        return remote(spot, spot, wzb_send.at[d], wzb_recv.at[d], me, mate)
+
+    own_shard = pltpu.make_async_copy(shard.at[own_rows], weight.at[x, z, own_rows], own.at[2])
+    own_shard.start()
+    for d in (4, 3, 5, 2, 6, 1, 7):
+        wza(d).start()
+    for d in (2, 1, 3):
+        wxb(d).start()
+
+    for d in (2, 1, 3, 0):
         for flip in range(2):
             if d == 0 and flip == 0:
                 continue
-            to_core = core if flip == 0 else 1 - core
-            for src, dst in upstream_parts(to_core):
+            of_core = core if flip == 0 else 1 - core
+            for src, dst in upstream_parts(of_core):
                 k = 2 * d + flip
-                remote(src, dst, u_send.at[k], u_recv.at[k], to_y * 2 + to_core, fs).start()
-    for src, dst in token_parts(y, tok_out):
+                remote(src, dst, u_send.at[k], u_recv.at[k], to_y(d) * 2 + of_core, fs).start()
+    for src, dst in token_parts(y, tok_in):
         pltpu.make_async_copy(src, dst, own.at[0]).start()
     for src, dst in upstream_parts(core):
         pltpu.make_async_copy(src, dst, own.at[1]).start()
 
-    def whole(send, recv, buf, slot):
-        return remote(buf.at[slot], buf.at[slot], send, recv, sibling, fs)
-
-    def both(send, recv, slot):
-        return remote(ups_out.at[:, slot], ups_out.at[:, slot], send, recv, sibling, fs)
+    def whole(send, recv, slot):
+        return remote(tok_in.at[slot], tok_in.at[slot], send, recv, sibling, fs)
+
+    def turn(slot):
+        tok_t[:, lanes(slot * 128, 128)] = tok_in[slot].T
+
+    pltpu.make_async_copy(tok_in.at[me], tok_in.at[me], own.at[0]).wait()
+    turn(me)
+    whole(f_send.at[0], f_recv.at[0], sibling).wait_recv()
+    turn(sibling)
+
+    own_shard.wait()
+    for d in (1, 3, 2):
+        wxb_in(d).wait_recv()
+    for d in (4, 3, 5, 2, 6, 1, 7):
+        wzb(d).start()
+    for d in (1, 7, 2, 6, 3, 5, 4):
+        wza_in(d).wait_recv()
+    for d in (2, 1, 3):
+        wxa(d).start()
 
     for d in (1, 3, 2):
         slot = lax.rem(y + 4 - d, 4) * 2 + core
-        whole(t_send.at[d], t_recv.at[d], tok_out, slot).wait_recv()
-        whole(f_send.at[d], f_recv.at[d], tok_out, slot).start()
-    for d in range(4):
+        whole(t_send.at[d], t_recv.at[d], slot).wait_recv()
+        whole(f_send.at[d], f_recv.at[d], slot).start()
+        turn(slot)
+    for d in (1, 3, 2):
         slot = lax.rem(y + 4 - d, 4) * 2 + 1 - core
-        whole(f_send.at[d], f_recv.at[d], tok_out, slot).wait()
-        if d:
-            whole(t_send.at[d], t_recv.at[d], tok_out, slot).wait_send()
-    for d in range(4):
+        whole(f_send.at[d], f_recv.at[d], slot).wait_recv()
+        turn(slot)
+    for d in (0, 1, 3, 2):
         for flip in range(2):
             if d == 0 and flip == 0:
                 continue
             from_core = core if flip == 0 else 1 - core
             slot = lax.rem(y + 4 - d, 4) * 2 + from_core
             k = 2 * d + flip
-            both(u_send.at[k], u_recv.at[k], slot).wait()
-    pltpu.make_async_copy(tok_out.at[me], tok_out.at[me], own.at[0]).wait()
-    pltpu.make_async_copy(ups_out.at[:, me], ups_out.at[:, me], own.at[1]).wait()
-
-
-def pool(tokens, upstream):
-    rows = tokens.shape[0]
-    dma = pltpu.SemaphoreType.DMA
-    return pl.pallas_call(
-        pool_kernel,
-        out_shape=(
-            jax.ShapeDtypeStruct((8, rows, 1024), jnp.bfloat16),
-            jax.ShapeDtypeStruct((2, 8, rows, 256), jnp.bfloat16),
-        ),
-        in_specs=[pl.BlockSpec(memory_space=pl.ANY)] * 2,
-        out_specs=(pl.BlockSpec(memory_space=pl.ANY),) * 2,
-        scratch_shapes=[dma((4,)), dma((4,)), dma((4,)), dma((4,)), dma((8,)), dma((8,)), dma((2,))],
-        compiler_params=pltpu.CompilerParams(
-            collective_id=0, has_side_effects=True, vmem_limit_bytes=VMEM_LIMIT
-        ),
-        cost_estimate=pl.CostEstimate(flops=0, bytes_accessed=64 << 20, transcendentals=0),
-    )(tokens, upstream)
-
-
-def sum_kernel(
-    table, part0, part1, block, outgoing, xbuf, xsum, zbuf, x_send, x_recv, z_send, z_recv, g_send, g_recv, f_send, f_recv
-):
-    me, fs = lax.axis_index("dp"), lax.axis_index("fsdp")
-    y, core, x, z = me // 2, me % 2, fs // 8, fs % 8
-    side = z % 2
-    sibling = y * 2 + 1 - core
-    mate = x * 8 + z + 1 - 2 * side
-
-    peers = [(me, lax.rem(x + d, 4) * 8 + z) for d in range(1, 4)]
-    peers += [(me, x * 8 + lax.rem(z + d, 8)) for d in range(1, 8)]
-    peers += [(lax.rem(y + d, 4) * 2 + core, fs) for d in range(1, 4)]
-    peers += [(lax.rem(y + d, 4) * 2 + core, mate) for d in range(1, 4)]
-    peers += [(sibling, fs)]
-    greet(peers)
-
-    def arrange(x_to):
+            spot = ups_in.at[:, slot]
+            remote(spot, spot, u_send.at[k], u_recv.at[k], sibling, fs).wait()
+    pltpu.make_async_copy(ups_in.at[:, me], ups_in.at[:, me], own.at[1]).wait()
+
+    def multiply(i, _):
+        rows = tok_t[pl.ds(pl.multiple_of(i * 256, 256), 256), :]
+        for b in range(2):
+            piece = jnp.dot(
+                rows, ups_in[b].reshape(1024, COLS), preferred_element_type=jnp.float32
+            )
+            part[b, 2 * i] = piece[:ROWS]
+            part[b, 2 * i + 1] = piece[ROWS:]
+        return 0
+
+    lax.fori_loop(0, 4, multiply, 0)
+
+    def arrange(of_x):
         def body(i, _):
-            g = x_to * 4 + i
-            chosen = table[g]
+            chosen = table[of_x * 4 + i]
             band = lax.div(chosen, 2)
-            piece = jnp.where(lax.rem(chosen, 2) == 0, part0[band], part1[band])
-            outgoing[2 * g] = piece[:HALF]
-            outgoing[2 * g + 1] = piece[HALF:]
+            piece = jnp.where(lax.rem(chosen, 2) == 0, part[0, band], part[1, band])
+            outgoing[of_x, 2 * i] = piece[:HALF]
+            outgoing[of_x, 2 * i + 1] = piece[HALF:]
             return 0
 
         lax.fori_loop(0, 4, body, 0)
 
-    def x_copy(d):
-        to = lax.rem(x + d, 4)
+    rows_a, rows_b = pl.ds(0, RA), pl.ds(RA, HALF - RA)
+
+    def xa(d):
         return remote(
-            outgoing.at[pl.ds(to * 8, 8)], xbuf.at[d], x_send.at[d], x_recv.at[d], me, to * 8 + z
+            outgoing.at[to_x(d), :, rows_a], xa_in.at[d], xa_send.at[d], xa_recv.at[d], me, to_x(d) * 8 + z
         )
 
+    def zb(d):
+        return remote(
+            outgoing.at[:, to_z(d), rows_b], zb_in.at[d], zb_send.at[d], zb_recv.at[d], me, x * 8 + to_z(d)
+        )
+
+    def za(d):
+        return remote(za_sum.at[to_z(d)], za_in.at[d], za_send.at[d], za_recv.at[d], me, x * 8 + to_z(d))
+
+    def xb(d):
+        return remote(xb_sum.at[to_x(d)], xb_in.at[d], xb_send.at[d], xb_recv.at[d], me, to_x(d) * 8 + z)
+
     for d in (2, 1, 3, 0):
-        arrange(lax.rem(x + d, 4))
+        arrange(to_x(d))
         if d:
-            x_copy(d).start()
+            xa(d).start()
+    for d in (4, 3, 5, 2, 6, 1, 7):
+        zb(d).start()
+
     for d in (1, 3, 2):
-        x_copy(d).wait_recv()
-
-    def z_copy(d):
-        to = lax.rem(z + d, 8)
-        return remote(xsum.at[to], zbuf.at[d], z_send.at[d], z_recv.at[d], me, x * 8 + to)
-
+        wxa_in(d).wait_recv()
+    for d in (1, 7, 2, 6, 3, 5, 4):
+        wzb_in(d).wait_recv()
+
+    def wy(d):
+        slab = weight.at[pl.ds(0 if d == 1 else 2, 2), :, own_rows]
+        return remote(slab, slab, wy_send.at[d], wy_recv.at[d], to_y(d) * 2 + core, fs)
+
+    def wy_in(d):
+        return weight.at[pl.ds(0 if d == 1 else 2, 2), :, other_rows]
+
+    def wc(k, spot):
+        return remote(spot, spot, wc_send.at[k], wc_recv.at[k], sibling, fs)
+
+    wy(1).start()
+    wy(3).start()
+    wc(0, weight.at[:, :, own_rows]).start()
+
+    for d in (1, 7, 2, 6, 3, 5, 4):
+        zb(d).wait_recv()
+    for d in (2, 1, 3, 0):
+        to = to_x(d)
+        total = outgoing[to, z, RA:]
+        for k in range(1, 8):
+            total = total + zb_in[k, to]
+        xb_sum[to] = total
+        if d:
+            xb(d).start()
+    for d in (1, 3, 2):
+        xa(d).wait_recv()
     for d in (4, 3, 5, 2, 6, 1, 7, 0):
-        to = lax.rem(z + d, 8)
-        xsum[to] = (outgoing[x * 8 + to] + xbuf[1, to]) + (xbuf[2, to] + xbuf[3, to])
+        to = to_z(d)
+        za_sum[to] = (outgoing[x, to, :RA] + xa_in[1, to]) + (xa_in[2, to] + xa_in[3, to])
         if d:
-            z_copy(d).start()
-    total = xsum[z]
+            za(d).start()
+
+    def place(of_y, of_side, of_core):
+        return block.at[
+            pl.ds(pl.multiple_of(of_y * ROWS + of_side * HALF, HALF), HALF), lanes(of_core * COLS, COLS)
+        ]
+
+    mine = place(y, side, core)
+    total = xb_sum[x]
+    for d in (1, 3, 2):
+        xb(d).wait_recv()
+        total = total + xb_in[d]
+    mine[rows_b] = total
+    total = za_sum[z]
     for d in (1, 7, 2, 6, 3, 5, 4):
-        z_copy(d).wait_recv()
-        total = total + zbuf[d]
-
-    def place(of_y, of_side, of_core):
-        return block.at[pl.ds(pl.multiple_of(of_y * ROWS + of_side * HALF, HALF), HALF), lanes(of_core * COLS, COLS)]
-
-    own = place(y, side, core)
-    own[...] = total
+        za(d).wait_recv()
+        total = total + za_in[d]
+    mine[rows_a] = total
 
     def g_copy(d, flip, spot):
-        fs_to = mate if flip else fs
         k = 2 * d + flip
-        return remote(spot, spot, g_send.at[k], g_recv.at[k], lax.rem(y + d, 4) * 2 + core, fs_to)
+        return remote(spot, spot, g_send.at[k], g_recv.at[k], to_y(d) * 2 + core, mate if flip else fs)
+
+    def h_copy(k, spot):
+        return remote(spot, spot, h_send.at[k], h_recv.at[k], sibling, fs)
 
     order = [(d, flip) for d in (2, 1, 3, 0) for flip in range(2) if d or flip]
     for d, flip in order:
-        g_copy(d, flip, own).start()
-
-    def f_copy(k, spot):
-        return remote(spot, spot, f_send.at[k], f_recv.at[k], sibling, fs)
-
-    f_copy(0, own).start()
+        g_copy(d, flip, mine).start()
+    h_copy(0, mine).start()
     for d, flip in reversed(order):
         spot = place(lax.rem(y + 4 - d, 4), 1 - side if flip else side, core)
         g_copy(d, flip, spot).wait_recv()
-        f_copy(2 * d + flip, spot).start()
+        h_copy(2 * d + flip, spot).start()
+
+    for d in (1, 3):
+        remote(wy_in(d), wy_in(d), wy_send.at[d], wy_recv.at[d], sibling, fs).wait_recv()
+        wc(d, wy_in(d)).start()
+
     for d in range(4):
         for flip in range(2):
             spot = place(lax.rem(y + 4 - d, 4), 1 - side if flip else side, 1 - core)
-            f_copy(2 * d + flip, spot).wait()
-    for d in (1, 2, 3):
-        x_copy(d).wait_send()
+            h_copy(2 * d + flip, spot).wait()
+
+    sib_rows = pl.ds(pl.multiple_of(64 * (y % 2) + 32 * (1 - core), 32), 32)
+    sib_other = pl.ds(pl.multiple_of(64 * (1 - y % 2) + 32 * (1 - core), 32), 32)
+    wc(0, weight.at[:, :, sib_rows]).wait()
+    for d in (1, 3):
+        wc(d, weight.at[pl.ds(0 if d == 1 else 2, 2), :, sib_other]).wait()
+
+    for d in range(1, 4):
+        whole(t_send.at[d], t_recv.at[d], me).wait_send()
+        xa(d).wait_send()
+        xb(d).wait_send()
+        wxa(d).wait_send()
+        wxb(d).wait_send()
+    for d in range(4):
+        whole(f_send.at[d], f_recv.at[d], me).wait_send()
     for d in range(1, 8):
-        z_copy(d).wait_send()
+        za(d).wait_send()
+        zb(d).wait_send()
+        wza(d).wait_send()
+        wzb(d).wait_send()
     for d, flip in order:
-        g_copy(d, flip, own).wait_send()
-
-
-def sum_blocks(table, parts):
+        g_copy(d, flip, mine).wait_send()
+    wy(1).wait_send()
+    wy(3).wait_send()
+
+
+def gradient_blocks(table, tokens, upstream, shard):
     dma = pltpu.SemaphoreType.DMA
-    f32 = jnp.float32
+    f32, b16 = jnp.float32, jnp.bfloat16
+    anywhere = pl.BlockSpec(memory_space=pl.ANY)
+    rows = tokens.shape[0]
     return pl.pallas_call(
-        sum_kernel,
-        out_shape=jax.ShapeDtypeStruct((BS, BS), f32),
-        in_specs=[pl.BlockSpec(memory_space=pltpu.SMEM)] + [pl.BlockSpec(memory_space=pltpu.VMEM)] * 2,
-        out_specs=pl.BlockSpec(memory_space=pltpu.VMEM),
+        gradient_kernel,
+        out_shape=(
+            jax.ShapeDtypeStruct((BS, BS), f32),
+            jax.ShapeDtypeStruct((NX, NZ, 128, 1024), b16),
+        ),
+        in_specs=[pl.BlockSpec(memory_space=pltpu.SMEM), anywhere, anywhere, anywhere],
+        out_specs=(pl.BlockSpec(memory_space=pltpu.VMEM), anywhere),
         scratch_shapes=[
-            pltpu.VMEM((32, HALF, COLS), f32),
-            pltpu.VMEM((4, 8, HALF, COLS), f32),
-            pltpu.VMEM((8, HALF, COLS), f32),
-            pltpu.VMEM((8, HALF, COLS), f32),
+            pltpu.VMEM((8, rows, 1024), b16),
+            pltpu.VMEM((1024, 8 * rows), b16),
+            pltpu.VMEM((2, 8, rows, COLS), b16),
+            pltpu.VMEM((2, 8, ROWS, COLS), f32),
+            pltpu.VMEM((NX, NZ, HALF, COLS), f32),
+            pltpu.VMEM((NX, NZ, RA, COLS), f32),
+            pltpu.VMEM((NZ, RA, COLS), f32),
+            pltpu.VMEM((NZ, RA, COLS), f32),
+            pltpu.VMEM((NZ, NX, HALF - RA, COLS), f32),
+            pltpu.VMEM((NX, HALF - RA, COLS), f32),
+            pltpu.VMEM((NX, HALF - RA, COLS), f32),
         ]
-        + [dma((4,)), dma((4,))]
-        + [dma((8,))] * 6,
+        + [dma((4,))] * 4
+        + [dma((8,))] * 2
+        + [dma((4,))] * 2
+        + [dma((8,))] * 4
+        + [dma((4,))] * 2
+        + [dma((8,))] * 4
+        + [dma((8,))] * 2
+        + [dma((4,))] * 2
+        + [dma((8,))] * 2
+        + [dma((4,))] * 6
+        + [dma((3,))],
         compiler_params=pltpu.CompilerParams(
             collective_id=1, has_side_effects=True, vmem_limit_bytes=VMEM_LIMIT
         ),
         cost_estimate=pl.CostEstimate(flops=0, bytes_accessed=64 << 20, transcendentals=0),
-    )(table, *parts)
+    )(table, tokens, upstream, shard)
 
 
 def finish_kernel(
@@ -412,19 +562,8 @@
 
 def local(tokens, upstream, weight, owner_table, stats_prev, roots_prev):
     dp, fs = lax.axis_index("dp"), lax.axis_index("fsdp")
-    full_weight = lax.all_gather(weight, "fsdp", axis=0, tiled=True)
-
-    tok_pool, ups_pool = pool(tokens, upstream)
-    parts = [
-        lax.dot_general(
-            tok_pool.reshape(-1, 1024),
-            ups_pool[b].reshape(-1, COLS),
-            (((0,), (0,)), ((), ())),
-            preferred_element_type=jnp.float32,
-        ).reshape(8, ROWS, COLS)
-        for b in range(2)
-    ]
-    grad_block = sum_blocks(owner_table, parts)
+    grad_block, full_weight = gradient_blocks(owner_table, tokens, upstream, weight)
+    full_weight = full_weight.reshape(-1, weight.shape[1])
     is_left = fs % 2 == 0
     root = newton(grad_block, stats_prev[0], roots_prev[0], is_left)
     left_rows = mm(lax.dynamic_slice_in_dim(root, dp * HALF, HALF, 0), grad_block)

time: 178 us -> 141 us (0.79)
  Pallas kernels: 129 us -> 104 us
  between operations: 14.9 us -> 1.45 us
  matrix products: 24.3 us -> 29 us
  local copies, waits for them, and re-layouts: 8.8 us -> 6.06 us
    pallas_call x2 -> x1, Pallas kernels: 105 us -> 79.9 us  [gradient_blocks(): pl.pallas_call(gradient_kernel, out_shape=(jax.ShapeDtypeStruct((BS, BS),...]
    dot_general x1, matrix products: 1.96 us -> 5.34 us  [local(): jnp.dot(tokens, full_weight, preferred_element_type=jnp.float32)]
    dot_general x10, matrix products: 13.5 us -> 16.4 us  [mm(): jnp.dot(left, right, precision=HIGH, preferred_element_type=jnp.float32)]
    dot_general x1 -> x0, local copies, waits for them, and re-layouts: 2.61 us -> none  [local(): lax.dot_general(tok_pool.reshape(-1, 1024), ups_pool[b].reshape(-1, COLS)...]
    unnamed x23 -> x19, local copies, waits for them, and re-layouts: 4.42 us -> 5.72 us
  transfers between devices with their start and end apart: 1 -> 0, of which waited for: 0 -> 0; matrix products, arithmetic and copies ran while one was open for 11% -> 0% of each run, Pallas kernels for 73% -> 0%
where the time goes in v2:
time: 141 us; the launch traced here: 140 us
  Pallas kernels  104 us (74%)
  matrix products  29 us (21%)
  local copies, waits for them, and re-layouts  6.06 us (4%)
  between operations  1.45 us (1%)
    pallas_call x1, Pallas kernels, gradient_blocks(): pl.pallas_call(gradient_kernel, out_shape=(jax.ShapeDtypeStruct((BS, BS),...  79.9 us
    pallas_call x1, Pallas kernels, finish(): pl.pallas_call(finish_kernel, out_shape=jax.ShapeDtypeStruct((128, 128),...  23.7 us
    dot_general x10, matrix products, mm(): jnp.dot(left, right, precision=HIGH, preferred_element_type=jnp.float32)  16.4 us
    dot_general x1, matrix products, local(): lax.dot_general(upstream, full_weight, (((1,), (1,)), ((), ())), preferre...  7.24 us
    unnamed x19, local copies, waits for them, and re-layouts  5.72 us
    dot_general x1, matrix products, local(): jnp.dot(tokens, full_weight, preferred_element_type=jnp.float32)  5.34 us

profile of v2, /device:TPU:8, one launch (start us, length us, event | category | flops | bytes accessed | tf_op | source)
XLA Modules:
  0.0 140.2 jit_solution(2363486239616409012)
XLA Ops:
  0.6 0.0 copy-start
  0.7 0.0 copy-start.1
  0.7 1.3 copy-done.1
  2.0 0.0 copy-start.4
  2.0 0.9 copy-done.4
  2.9 0.0 copy-start.6
  2.9 0.9 copy-done.6
  3.9 0.0 copy-start.7
  3.9 0.7 copy-done.7
  4.5 79.9 %shard_map.93 = (f32[512,512]{1,0:T(8,128)S(1)}, bf16[4,8,128,1024]{3,2,1,0:T(8,128)(2,1)}) custom-call(s32[16]{0:T(128)S(1)} %copy-done.7, bf16[128,4096]{1,0:T(8,128)(2,1)S(1)} %copy-done.1, bf16[128,1024]{1,0:T(8,128)(2,1)S(1)} %copy-done.4, bf16[128,1024]{1,0:T(8,128)(2,1)S(1)} %copy-done.6), custom_call_target="tpu_custom_call" | custom-call | bytes 67108864 | tf_op jit(solution)/shard_map/pallas_call | solution.py:350
  84.5 0.3 copy.11
  84.8 3.9 %select_reduce_fusion = (f32[]{:T(128)}, f32[512,512]{1,0:T(8,128)}) fusion(f32[512,512]{1,0:T(8,128)S(1)} %get-tuple-element.9, f32[512,512]{0,1:T(8,128)S(1)} %copy.11, pred[]{:T(512)S(6)} %eq.31, f32[1,512,512]{2,1,0:T(8,128)} %param.10), kind=kOutput, calls=%fused_computation.15 | convolution fusion | flops 807141376 | bytes 4194309 | tf_op jit(solution)/shard_map/dot_general | solution.py:544
  89.3 0.0 copy-done
  89.3 1.0 fusion.5
  90.4 1.0 fusion.29
  91.4 2.2 %fusion.7 = f32[512,512]{1,0:T(8,128)S(1)} fusion(f32[512,512]{1,0:T(8,128)S(1)} %fusion.29, f32[512,512]{1,0:T(8,128)} %get-tuple-element.15, f32[]{:T(128)S(6)} %div.9), kind=kOutput, calls=%fused_computation.13 | convolution fusion | flops 805568512 | bytes 3145732 | tf_op jit(solution)/shard_map/dot_general | solution.py:544
  93.6 0.0 copy-start.8
  93.6 0.0 copy-start.5
  93.7 1.0 fusion.9
  94.7 1.0 fusion.30
  95.7 1.0 fusion.1
  96.7 1.9 %fusion.3 = f32[512,512]{1,0:T(8,128)S(1)} fusion(f32[1,512,512]{2,1,0:T(8,128)S(1)} %copy-done, f32[512,512]{1,0:T(8,128)S(1)} %fusion.7), kind=kOutput, calls=%fused_computation.9 | convolution fusion | flops 806354944 | bytes 3145728 | tf_op jit(solution)/shard_map/dot_general | solution.py:544
  98.6 0.0 copy-start.2
  98.6 2.0 %fusion.31.root = f32[512,512]{1,0:T(8,128)} fusion(f32[512,512]{1,0:T(8,128)S(1)} %fusion.3, f32[512,512]{1,0:T(8,128)S(1)} %fusion.1), kind=kOutput, calls=%fused_computation.39 | convolution fusion | flops 805306368 | bytes 3145728 | tf_op jit(solution)/shard_map/dot_general | solution.py:544
  100.6 1.3 fusion.20.left_rows
  101.9 0.0 copy-done.8
  102.0 0.1 select_reduce_fusion.1.inverse
  102.1 0.0 copy-start.3
  102.1 1.2 copy-done.3
  103.3 23.7 %shard_map.94 = bf16[128,128]{1,0:T(8,128)(2,1)S(1)} custom-call(s32[16]{0:T(128)S(1)} %select_reduce_fusion.1.inverse, f32[64,512]{1,0:T(8,128)S(1)} %fusion.20.left_rows, f32[512,512]{1,0:T(8,128)S(1)} %copy-done.3), custom_call_target="tpu_custom_call" | custom-call | bytes 33554432 | tf_op jit(solution)/shard_map/pallas_call | solution.py:515
  127.0 0.0 copy-done.5
  127.0 7.2 %convolution_convert_fusion = bf16[128,4096]{1,0:T(8,128)(2,1)} fusion(bf16[128,1024]{1,0:T(8,128)(2,1)S(1)} %copy-done.5, bf16[4096,1024]{1,0:T(8,128)(2,1)} %bitcast.29), kind=kOutput, calls=%fused_computation | convolution fusion | flops 1074266112 | bytes 9699328 | tf_op jit(solution)/shard_map/dot_general | solution.py:578
  134.3 0.0 copy-done.2
  134.3 5.3 %convolution_convert_fusion.1 = bf16[128,1024]{1,0:T(8,128)(2,1)} fusion(bf16[128,4096]{1,0:T(8,128)(2,1)S(1)} %copy-done.2, bf16[4096,1024]{1,0:T(8,128)(2,1)} %bitcast.30), kind=kOutput, calls=%fused_computation.6 | convolution fusion | flops 1073872896 | bytes 9699328 | tf_op jit(solution)/shard_map/dot_general | solution.py:577
  139.6 0.6 copy.13
Async XLA Ops:
  0.6 88.7 %copy-start = (f32[1,512,512]{2,1,0:T(8,128)S(1)}, f32[1,512,512]{2,1,0:T(8,128)}, u32[]{:S(2)}) copy-start(f32[1,512,512]{2,1,0:T(8,128)} %param.11) | copy-start | bytes 3145732
  0.7 1.3 copy-start.1
  2.0 0.9 copy-start.4
  2.9 0.9 copy-start.6
  3.9 0.7 copy-start.7
  93.6 8.3 %copy-start.8 = (s32[16]{0:T(128)S(1)}, s32[16]{0:T(128)}, u32[]{:S(2)}) copy-start(s32[16]{0:T(128)} %table.1) | copy-start | bytes 196
  93.6 33.4 %copy-start.5 = (bf16[128,1024]{1,0:T(8,128)(2,1)S(1)}, bf16[128,1024]{1,0:T(8,128)(2,1)}, u32[]{:S(2)}) copy-start(bf16[128,1024]{1,0:T(8,128)(2,1)} %ups.1) | copy-start | bytes 786436
  98.6 35.7 %copy-start.2 = (bf16[128,4096]{1,0:T(8,128)(2,1)S(1)}, bf16[128,4096]{1,0:T(8,128)(2,1)}, u32[]{:S(2)}) copy-start(bf16[128,4096]{1,0:T(8,128)(2,1)} %tok.1) | copy-start | bytes 3145732
  102.1 1.2 copy-start.3

commit v3 on v2

--- a/solution.py
+++ b/solution.py
@@ -1,5 +1,3 @@
-import functools
-
 import jax
 import jax.numpy as jnp
 from jax import lax
@@ -7,11 +5,10 @@
 from jax.experimental.pallas import tpu as pltpu
 from jax.sharding import PartitionSpec as P
 
-HIGH = lax.Precision.HIGH
 STAT_DECAY = 0.8
 NORM_EPSILON = 1e-06
 MESH = pl.DeviceIdType.MESH
-VMEM_LIMIT = 48 * 1024 * 1024
+VMEM_LIMIT = 60 * 1024 * 1024
 
 NX, NY, NZ = 4, 4, 8
 BS = 512
@@ -34,25 +31,34 @@
     )
 
 
-def greet(peers):
-    barrier = pltpu.get_barrier_semaphore()
-    for dp, fsdp in peers:
-        pl.semaphore_signal(barrier, inc=1, device_id=(dp, fsdp), device_id_type=MESH)
-    pl.semaphore_wait(barrier, len(peers))
-
-
 def lanes(start, size):
     return pl.ds(pl.multiple_of(start, 128), size)
 
 
-def gradient_kernel(
-    table, tok, ups, shard, block, weight,
+def dot3(left, right, contract=((1,), (0,))):
+    def split(a):
+        high = a.astype(jnp.bfloat16)
+        return high, (a - high.astype(jnp.float32)).astype(jnp.bfloat16)
+
+    def one(a, b):
+        return lax.dot_general(a, b, (contract, ((), ())), preferred_element_type=jnp.float32)
+
+    (lh, ll), (rh, rl) = split(left), split(right)
+    return one(lh, rh) + (one(lh, rl) + one(ll, rh))
+
+
+def update_kernel(
+    table, tok, ups, shard, stats_prev, root_prev,
+    projected, input_grad, root, out,
+    block, weight, tok_own, ups_own, stats, start, square, fourth, moment, factor, iterate,
+    projected_sum, rows_out, rows_in, energies, chunks, spread, picked,
     tok_in, tok_t, ups_in, part, outgoing, xa_in, za_sum, za_in, zb_in, xb_sum, xb_in,
     t_send, t_recv, f_send, f_recv, u_send, u_recv,
     xa_send, xa_recv, za_send, za_recv, zb_send, zb_recv, xb_send, xb_recv,
     g_send, g_recv, h_send, h_recv,
     wza_send, wza_recv, wxa_send, wxa_recv, wzb_send, wzb_recv, wxb_send, wxb_recv,
     wy_send, wy_recv, wc_send, wc_recv, own,
+    a_send, a_recv, e_send, e_recv, s_send, s_recv, p_send, p_recv,
 ):
     me, fs = lax.axis_index("dp"), lax.axis_index("fsdp")
     y, core, x, z = me // 2, me % 2, fs // 8, fs % 8
@@ -73,7 +79,54 @@
     peers += [(me, to_x(d) * 8 + z) for d in range(1, 4)]
     peers += [(me, x * 8 + to_z(d)) for d in range(1, 8)]
     peers += [(to_y(d) * 2 + core, mate) for d in range(1, 4)]
-    greet(peers)
+
+    group, piece = fs // 2, z % 4
+    sources = [(2 * piece + i, 2 * (4 * q + me % 4) + 1, i, q) for i in range(2) for q in range(4)]
+    my_quarter, my_cols = group // 4, group % 4
+    places = [
+        (4 * b + my_cols, 4 * r + me // 2, 2 * r + b) for r in range(8) for b in range(2)
+    ]
+
+    def away(dp, fsdp):
+        return jnp.logical_or(dp != me, fsdp != fs)
+
+    barrier = pltpu.get_barrier_semaphore()
+
+    def tell(dp, fsdp):
+        pl.semaphore_signal(barrier, inc=1, device_id=(dp, fsdp), device_id_type=MESH)
+
+    for dp, fsdp, _, _ in sources:
+        @pl.when(away(dp, fsdp))
+        def _(dp=dp, fsdp=fsdp):
+            tell(dp, fsdp)
+
+    @pl.when(side == 1)
+    def _():
+        for d in range(1, NB):
+            tell(me, lax.rem(fs + 2 * d, 32))
+
+    for dp, fsdp in peers:
+        tell(dp, fsdp)
+
+    local = [
+        pltpu.make_async_copy(root_prev, start, own.at[3]),
+        pltpu.make_async_copy(stats_prev, stats, own.at[4]),
+        pltpu.make_async_copy(tok, tok_own, own.at[5]),
+        pltpu.make_async_copy(ups, ups_own, own.at[6]),
+    ]
+    for copy in local:
+        copy.start()
+
+    @pl.when(side == 0)
+    def _():
+        pl.semaphore_wait(barrier, len(peers))
+
+    @pl.when(side == 1)
+    def _():
+        at_home = jnp.int32(0)
+        for dp, fsdp, _ in places:
+            at_home += jnp.where(away(dp, fsdp), 0, 1)
+        pl.semaphore_wait(barrier, len(peers) + NB - 1 + NB - at_home)
 
     def token_parts(of_y, where):
         for r in range(8):
@@ -160,6 +213,9 @@
     whole(f_send.at[0], f_recv.at[0], sibling).wait_recv()
     turn(sibling)
 
+    local[0].wait()
+    square[...] = dot3(start[...], start[...])
+
     own_shard.wait()
     for d in (1, 3, 2):
         wxb_in(d).wait_recv()
@@ -169,6 +225,8 @@
         wza_in(d).wait_recv()
     for d in (2, 1, 3):
         wxa(d).start()
+
+    fourth[...] = dot3(square[...], square[...])
 
     for d in (1, 3, 2):
         slot = lax.rem(y + 4 - d, 4) * 2 + core
@@ -317,11 +375,157 @@
             spot = place(lax.rem(y + 4 - d, 4), 1 - side if flip else side, 1 - core)
             h_copy(2 * d + flip, spot).wait()
 
+    local[1].wait()
+
+    @pl.when(side == 0)
+    def _():
+        moment[...] = dot3(block[...], block[...], ((1,), (1,)))
+
+    @pl.when(side == 1)
+    def _():
+        moment[...] = dot3(block[...], block[...], ((0,), (0,)))
+
+    diagonal = lax.broadcasted_iota(jnp.int32, (BS, BS), 0) == lax.broadcasted_iota(jnp.int32, (BS, BS), 1)
+    fresh = STAT_DECAY * stats[...] + (1.0 - STAT_DECAY) * moment[...]
+    trace = jnp.sum(jnp.where(diagonal, fresh, 0.0))
+    stats[...] = fresh / (trace / BS)
+
+    def next_factor():
+        return (jnp.where(diagonal, 5.0, 0.0) - moment[...]) * 0.25
+
+    moment[...] = dot3(fourth[...], stats[...])
+    factor[...] = next_factor()
+    square[...] = dot3(factor[...], factor[...])
+    fourth[...] = dot3(square[...], square[...])
+    iterate[...] = dot3(start[...], factor[...])
+    moment[...] = dot3(fourth[...], moment[...])
+    factor[...] = next_factor()
+    root[...] = dot3(iterate[...], factor[...])
+
     sib_rows = pl.ds(pl.multiple_of(64 * (y % 2) + 32 * (1 - core), 32), 32)
     sib_other = pl.ds(pl.multiple_of(64 * (1 - y % 2) + 32 * (1 - core), 32), 32)
     wc(0, weight.at[:, :, sib_rows]).wait()
     for d in (1, 3):
         wc(d, weight.at[pl.ds(0 if d == 1 else 2, 2), :, sib_other]).wait()
+    local[2].wait()
+    local[3].wait()
+
+    def products(i):
+        band = weight[i].reshape(1024, 1024)
+        here = jnp.dot(tok_own[:, 1024 * i : 1024 * i + 1024], band, preferred_element_type=jnp.float32)
+        if i:
+            here = here + projected_sum[...]
+        if i < 3:
+            projected_sum[...] = here
+        else:
+            projected[...] = here.astype(jnp.bfloat16)
+        input_grad[:, 1024 * i : 1024 * i + 1024] = lax.dot_general(
+            ups_own[...], band, (((1,), (1,)), ((), ())), preferred_element_type=jnp.float32
+        ).astype(jnp.bfloat16)
+
+    def a_copy():
+        return remote(rows_out, rows_in, a_send, a_recv, me, mate)
+
+    def e_copy(d):
+        return remote(energies.at[0], energies.at[d], e_send.at[d], e_recv.at[d], lax.rem(me + d, 8), fs)
+
+    def s_copy(d):
+        to = lax.rem(group + d, NB)
+        return remote(chunks.at[to], spread.at[group], s_send.at[d], s_recv.at[d], me, 2 * to + 1)
+
+    def out_rows(i, q):
+        return out.at[pl.ds(pl.multiple_of(HALF * i + 16 * q, 16), 16)]
+
+    def p_copy(dp, fsdp, b):
+        return remote(
+            picked.at[b], out_rows(me % 2, my_quarter), p_send.at[b],
+            p_recv.at[4 * (me % 2) + my_quarter], dp, fsdp,
+        )
+
+    def p_home(b):
+        return pltpu.make_async_copy(picked.at[b], out_rows(me % 2, my_quarter), own.at[7])
+
+    @pl.when(side == 0)
+    def _():
+        rows_out[...] = dot3(root[pl.ds(pl.multiple_of(me * HALF, HALF), HALF), :], block[...])
+        a_copy().start()
+
+    @pl.when(side == 1)
+    def _():
+        a_copy().wait_recv()
+        iterate[:HALF] = dot3(rows_in[...], root[...])
+        product = iterate[:HALF]
+        energies[0] = jnp.full((8, 128), jnp.sum(product * product), jnp.float32)
+        for d in range(1, 8):
+            e_copy(d).start()
+
+    products(0)
+
+    @pl.when(side == 1)
+    def _():
+        for d in range(1, 8):
+            e_copy(d).wait_recv()
+        total = jnp.zeros((8, 128), jnp.float32)
+        for dp in range(8):
+            total = total + energies[lax.rem(me - dp + 8, 8)]
+        mean = total[0:1, 0:1] / (BS * BS)
+        update = (iterate[:HALF] / jnp.sqrt(mean + NORM_EPSILON)).astype(jnp.bfloat16)
+        for j in range(NB):
+            q, c = j // 4, j % 4
+            chunks[j] = update[16 * q : 16 * q + 16, 128 * c : 128 * c + 128]
+        for d in (8, 7, 9, 6, 10, 5, 11, 4, 12, 3, 13, 2, 14, 1, 15):
+            s_copy(d).start()
+        spread[group] = chunks[group]
+
+    products(1)
+    products(2)
+
+    @pl.when(side == 1)
+    def _():
+        for d in range(1, NB):
+            source = lax.rem(group + NB - d, NB)
+            remote(
+                chunks.at[0], spread.at[source], s_send.at[d], s_recv.at[d], me, 2 * source + 1
+            ).wait_recv()
+        for dp, fsdp, b in places:
+            holder = jnp.int32(0)
+            for g in range(1, NB):
+                holder = jnp.maximum(holder, jnp.where(table[g] == b, g, 0))
+            picked[b] = spread[holder]
+
+            @pl.when(away(dp, fsdp))
+            def _(dp=dp, fsdp=fsdp, b=b):
+                p_copy(dp, fsdp, b).start()
+
+            @pl.when(jnp.logical_not(away(dp, fsdp)))
+            def _(b=b):
+                p_home(b).start()
+
+    products(3)
+
+    for dp, fsdp, i, q in sources:
+        @pl.when(away(dp, fsdp))
+        def _(dp=dp, fsdp=fsdp, i=i, q=q):
+            remote(picked.at[0], out_rows(i, q), p_send.at[0], p_recv.at[4 * i + q], dp, fsdp).wait_recv()
+
+    @pl.when(side == 0)
+    def _():
+        a_copy().wait_send()
+
+    @pl.when(side == 1)
+    def _():
+        for d in range(1, 8):
+            e_copy(d).wait_send()
+        for d in range(1, NB):
+            s_copy(d).wait_send()
+        for dp, fsdp, b in places:
+            @pl.when(away(dp, fsdp))
+            def _(dp=dp, fsdp=fsdp, b=b):
+                p_copy(dp, fsdp, b).wait_send()
+
+            @pl.when(jnp.logical_not(away(dp, fsdp)))
+            def _(b=b):
+                p_home(b).wait()
 
     for d in range(1, 4):
         whole(t_send.at[d], t_recv.at[d], me).wait_send()
@@ -342,20 +546,37 @@
     wy(3).wait_send()
 
 
-def gradient_blocks(table, tokens, upstream, shard):
+def update(table, tokens, upstream, shard, stats_prev, root_prev):
     dma = pltpu.SemaphoreType.DMA
     f32, b16 = jnp.float32, jnp.bfloat16
-    anywhere = pl.BlockSpec(memory_space=pl.ANY)
+    anywhere, vmem = pl.BlockSpec(memory_space=pl.ANY), pl.BlockSpec(memory_space=pltpu.VMEM)
     rows = tokens.shape[0]
+    square = pltpu.VMEM((BS, BS), f32)
     return pl.pallas_call(
-        gradient_kernel,
+        update_kernel,
         out_shape=(
+            jax.ShapeDtypeStruct((rows, 1024), b16),
+            jax.ShapeDtypeStruct((rows, 4096), b16),
             jax.ShapeDtypeStruct((BS, BS), f32),
-            jax.ShapeDtypeStruct((NX, NZ, 128, 1024), b16),
+            jax.ShapeDtypeStruct((128, 128), b16),
         ),
-        in_specs=[pl.BlockSpec(memory_space=pltpu.SMEM), anywhere, anywhere, anywhere],
-        out_specs=(pl.BlockSpec(memory_space=pltpu.VMEM), anywhere),
+        in_specs=[pl.BlockSpec(memory_space=pltpu.SMEM)] + [anywhere] * 5,
+        out_specs=(vmem,) * 4,
         scratch_shapes=[
+            square,
+            pltpu.VMEM((NX, NZ, 128, 1024), b16),
+            pltpu.VMEM((rows, 4096), b16),
+            pltpu.VMEM((rows, 1024), b16),
+        ]
+        + [square] * 7
+        + [
+            pltpu.VMEM((rows, 1024), f32),
+            pltpu.VMEM((HALF, BS), f32),
+            pltpu.VMEM((HALF, BS), f32),
+            pltpu.VMEM((8, 8, 128), f32),
+            pltpu.VMEM((NB, 16, 128), b16),
+            pltpu.VMEM((NB, 16, 128), b16),
+            pltpu.VMEM((NB, 16, 128), b16),
             pltpu.VMEM((8, rows, 1024), b16),
             pltpu.VMEM((1024, 8 * rows), b16),
             pltpu.VMEM((2, 8, rows, COLS), b16),
@@ -378,206 +599,40 @@
         + [dma((4,))] * 2
         + [dma((8,))] * 2
         + [dma((4,))] * 6
-        + [dma((3,))],
+        + [dma((8,)), dma(()), dma(()), dma((8,)), dma((8,))]
+        + [dma((NB,))] * 3
+        + [dma((8,))],
         compiler_params=pltpu.CompilerParams(
-            collective_id=1, has_side_effects=True, vmem_limit_bytes=VMEM_LIMIT
+            collective_id=0, has_side_effects=True, vmem_limit_bytes=VMEM_LIMIT
         ),
         cost_estimate=pl.CostEstimate(flops=0, bytes_accessed=64 << 20, transcendentals=0),
-    )(table, tokens, upstream, shard)
-
-
-def finish_kernel(
-    inverse, left_rows, root, out, rows_in, energies, chunks, spread, picked,
-    a_send, a_recv, e_send, e_recv, s_send, s_recv, p_send, p_recv, local
-):
-    me, fs = lax.axis_index("dp"), lax.axis_index("fsdp")
-    z = fs % 8
-    group, side = fs // 2, z % 2
-    piece = z % 4
-    sources = [(2 * piece + i, 2 * (4 * q + me % 4) + 1, i, q) for i in range(2) for q in range(4)]
-    my_piece, my_quarter, my_cols = me // 2, group // 4, group % 4
-    places = [
-        (4 * cb + my_cols, 4 * rb + my_piece, 2 * rb + cb) for rb in range(8) for cb in range(2)
-    ]
-    barrier = pltpu.get_barrier_semaphore()
-
-    def tell(dp, fsdp):
-        pl.semaphore_signal(barrier, inc=1, device_id=(dp, fsdp), device_id_type=MESH)
-
-    for dp, fsdp, _, _ in sources:
-        @pl.when(jnp.logical_or(dp != me, fsdp != fs))
-        def _(dp=dp, fsdp=fsdp):
-            tell(dp, fsdp)
-
-    def out_rows(i, q):
-        return out.at[pl.ds(pl.multiple_of(HALF * i + 16 * q, 16), 16)]
-
-    def a_copy():
-        return remote(left_rows, rows_in, a_send, a_recv, me, fs + 1 - 2 * side)
-
-    @pl.when(side == 0)
-    def _():
-        pl.semaphore_wait(barrier, 1)
-        a_copy().start()
-        a_copy().wait_send()
-
-    @pl.when(side == 1)
-    def _():
-        tell(me, fs - 1)
-        for d in range(1, 8):
-            tell(lax.rem(me + d, 8), fs)
-        for d in range(1, NB):
-            tell(me, lax.rem(fs + 2 * d, 32))
-        is_own = jnp.int32(0)
-        for dp, fsdp, _ in places:
-            is_own += jnp.where(jnp.logical_and(dp == me, fsdp == fs), 1, 0)
-        pl.semaphore_wait(barrier, 7 + 15 + 16 - is_own)
-
-        a_copy().wait_recv()
-        product = jnp.dot(
-            rows_in[...], root[...], precision=lax.Precision.HIGHEST, preferred_element_type=jnp.float32
-        )
-        energy = jnp.sum(product * product)
-        energies[0] = jnp.full((8, 128), energy, jnp.float32)
-
-        def e_copy(d):
-            return remote(
-                energies.at[0], energies.at[d], e_send.at[d], e_recv.at[d], lax.rem(me + d, 8), fs
-            )
-
-        for d in range(1, 8):
-            e_copy(d).start()
-        for d in range(1, 8):
-            e_copy(d).wait_recv()
-
-        total = jnp.zeros((8, 128), jnp.float32)
-        for dp in range(8):
-            total = total + energies[lax.rem(me - dp + 8, 8)]
-        mean = total[0:1, 0:1] / (BS * BS)
-        update = (product / jnp.sqrt(mean + NORM_EPSILON)).astype(jnp.bfloat16)
-        for j in range(NB):
-            q, k = j // 4, j % 4
-            chunks[j] = update[16 * q : 16 * q + 16, 128 * k : 128 * k + 128]
-
-        def s_copy(d):
-            to = lax.rem(group + d, NB)
-            return remote(
-                chunks.at[to], spread.at[group], s_send.at[d], s_recv.at[d], me, 2 * to + 1
-            )
-
-        for d in range(1, NB):
-            s_copy(d).start()
-        spread[group] = chunks[group]
-        for d in range(1, NB):
-            source = lax.rem(group + NB - d, NB)
-            remote(
-                chunks.at[0], spread.at[source], s_send.at[d], s_recv.at[d], me, 2 * source + 1
-            ).wait_recv()
-        for dp, fsdp, b in places:
-            picked[b] = spread[inverse[b]]
-
-        def p_copy(dp, fsdp, b):
-            i, q = me % 2, my_quarter
-            return remote(picked.at[b], out_rows(i, q), p_send.at[b], p_recv.at[4 * i + q], dp, fsdp)
-
-        for dp, fsdp, b in places:
-            mine = jnp.logical_and(dp == me, fsdp == fs)
-
-            @pl.when(mine)
-            def _(b=b):
-                copy = pltpu.make_async_copy(picked.at[b], out_rows(me % 2, my_quarter), local)
-                copy.start()
-                copy.wait()
-
-            @pl.when(jnp.logical_not(mine))
-            def _(dp=dp, fsdp=fsdp, b=b):
-                p_copy(dp, fsdp, b).start()
-
-        for d in range(1, 8):
-            e_copy(d).wait_send()
-        for d in range(1, NB):
-            s_copy(d).wait_send()
-        for dp, fsdp, b in places:
-            @pl.when(jnp.logical_or(dp != me, fsdp != fs))
-            def _(dp=dp, fsdp=fsdp, b=b):
-                p_copy(dp, fsdp, b).wait_send()
-
-    for dp, fsdp, i, q in sources:
-        @pl.when(jnp.logical_or(dp != me, fsdp != fs))
-        def _(dp=dp, fsdp=fsdp, i=i, q=q):
-            remote(picked.at[0], out_rows(i, q), p_send.at[0], p_recv.at[4 * i + q], dp, fsdp).wait_recv()
-
-
-def finish(inverse, left_rows, root):
-    dma = pltpu.SemaphoreType.DMA
-    f32, b16 = jnp.float32, jnp.bfloat16
-    vmem = pl.BlockSpec(memory_space=pltpu.VMEM)
+    )(table, tokens, upstream, shard, stats_prev, root_prev)
+
+
+def settle_kernel(*refs):
+    n = len(refs) // 2
+    copies = [pltpu.make_async_copy(refs[i], refs[n + i], refs[-1].at[i]) for i in range(n)]
+    for copy in copies:
+        copy.start()
+    for copy in copies:
+        copy.wait()
+
+
+def settle(*arrays):
+    anywhere = pl.BlockSpec(memory_space=pl.ANY)
     return pl.pallas_call(
-        finish_kernel,
-        out_shape=jax.ShapeDtypeStruct((128, 128), b16),
-        in_specs=[pl.BlockSpec(memory_space=pltpu.SMEM), vmem, vmem],
-        out_specs=vmem,
-        scratch_shapes=[
-            pltpu.VMEM((HALF, BS), f32),
-            pltpu.VMEM((8, 8, 128), f32),
-            pltpu.VMEM((NB, 16, 128), b16),
-            pltpu.VMEM((NB, 16, 128), b16),
-            pltpu.VMEM((NB, 16, 128), b16),
-            dma(()),
-            dma(()),
-            dma((8,)),
-            dma((8,)),
-            dma((NB,)),
-            dma((NB,)),
-            dma((NB,)),
-            dma((8,)),
-            dma(()),
-        ],
-        compiler_params=pltpu.CompilerParams(
-            collective_id=2, has_side_effects=True, vmem_limit_bytes=VMEM_LIMIT
-        ),
-        cost_estimate=pl.CostEstimate(flops=0, bytes_accessed=32 << 20, transcendentals=0),
-    )(inverse, left_rows, root)
-
-
-def mm(left, right):
-    return jnp.dot(left, right, precision=HIGH, preferred_element_type=jnp.float32)
-
-
-def newton(grad_block, stats_prev, root_prev, is_left):
-    chosen = jnp.where(is_left, grad_block, grad_block.T)
-    gram = mm(chosen, chosen.T)
-    stats = STAT_DECAY * stats_prev + (1.0 - STAT_DECAY) * gram
-    normed = stats / (jnp.trace(stats) / BS)
-    identity = jnp.eye(BS, dtype=jnp.float32)
-    square = mm(root_prev, root_prev)
-    moment = mm(mm(square, square), normed)
-    factor = (5.0 * identity - moment) * 0.25
-    iterate = mm(root_prev, factor)
-    factor_sq = mm(factor, factor)
-    moment = mm(mm(factor_sq, factor_sq), moment)
-    factor = (5.0 * identity - moment) * 0.25
-    return mm(iterate, factor)
+        settle_kernel,
+        out_shape=tuple(jax.ShapeDtypeStruct(a.shape, a.dtype) for a in arrays),
+        in_specs=[anywhere] * len(arrays),
+        out_specs=(anywhere,) * len(arrays),
+        scratch_shapes=[pltpu.SemaphoreType.DMA((len(arrays),))],
+    )(*arrays)
 
 
 def local(tokens, upstream, weight, owner_table, stats_prev, roots_prev):
-    dp, fs = lax.axis_index("dp"), lax.axis_index("fsdp")
-    grad_block, full_weight = gradient_blocks(owner_table, tokens, upstream, weight)
-    full_weight = full_weight.reshape(-1, weight.shape[1])
-    is_left = fs % 2 == 0
-    root = newton(grad_block, stats_prev[0], roots_prev[0], is_left)
-    left_rows = mm(lax.dynamic_slice_in_dim(root, dp * HALF, HALF, 0), grad_block)
-    positions = jnp.arange(NB, dtype=jnp.int32)
-    inverse = jnp.sum(
-        jnp.where(owner_table[None, :] == positions[:, None], positions[None, :], 0), axis=1
+    projected, input_grad, root, direction = settle(
+        *update(owner_table, tokens, upstream, weight, stats_prev[0], roots_prev[0])
     )
-    direction = finish(inverse, left_rows, root)
-
-    tokens, upstream, direction = lax.optimization_barrier((tokens, upstream, direction))
-    projected = jnp.dot(tokens, full_weight, preferred_element_type=jnp.float32).astype(jnp.bfloat16)
-    input_grad = lax.dot_general(
-        upstream, full_weight, (((1,), (1,)), ((), ())), preferred_element_type=jnp.float32
-    ).astype(jnp.bfloat16)
     return projected, input_grad, root[None], direction
 
 

time: 141 us -> 185 us (1.31)
  Pallas kernels: 104 us -> 184 us
  matrix products: 29 us -> 0 us
  local copies, waits for them, and re-layouts: 6.06 us -> 0 us
    pallas_call x2, Pallas kernels: 104 us -> 184 us  [the longest x1 110 us: update(): pl.pallas_call(update_kernel, out_shape=(jax.ShapeDtypeStruct((rows, 1024...]
    dot_general x12 -> x0, matrix products: 29 us -> none  [the longest x10 16.4 us: mm(): jnp.dot(left, right, precision=HIGH, preferred_element_type=jnp.float32)]
    unnamed x19 -> x0, local copies, waits for them, and re-layouts: 5.72 us -> none
where the time goes in v3:
time: 185 us; the launch traced here: 184 us
  Pallas kernels  184 us (99%)
    pallas_call x1, Pallas kernels, update(): pl.pallas_call(update_kernel, out_shape=(jax.ShapeDtypeStruct((rows, 1024...  110 us
    pallas_call x1, Pallas kernels, settle(): pl.pallas_call(settle_kernel, out_shape=tuple((jax.ShapeDtypeStruct(a.sha...  73.6 us

profile of v3, /device:TPU:8, one launch (start us, length us, event | category | flops | bytes accessed | tf_op | source)
XLA Modules:
  0.0 184.4 jit_solution(5208306695758630710)
XLA Ops:
  0.6 110.2 %shard_map.93 = (bf16[128,1024]{1,0:T(8,128)(2,1)}, bf16[128,4096]{1,0:T(8,128)(2,1)}, f32[512,512]{1,0:T(8,128)}, bf16[128,128]{1,0:T(8,128)(2,1)}) custom-call(s32[16]{0:T(128)} %table.1, bf16[128,4096]{1,0:T(8,128)(2,1)} %tok.1, bf16[128,1024]{1,0:T(8,128)(2,1)} %ups.1, bf16[128,1024]{1,0:T(8,128)(2,1)} %shard.1, f32[512,512]{1,0:T(8,128)} %bitcast.3, ...), custom_call_target="tpu_custom_call" | custom-call | bytes 67108864 | tf_op jit(solution)/shard_map/pallas_call | solution.py:555
  110.8 73.6 %shard_map.94 = (bf16[128,1024]{1,0:T(8,128)(2,1)}, bf16[128,4096]{1,0:T(8,128)(2,1)}, f32[512,512]{1,0:T(8,128)}, bf16[128,128]{1,0:T(8,128)(2,1)}) custom-call(bf16[128,1024]{1,0:T(8,128)(2,1)} %get-tuple-element.12.refs_0_, bf16[128,4096]{1,0:T(8,128)(2,1)} %get-tuple-element.13.refs_1_, f32[512,512]{1,0:T(8,128)} %get-tuple-element.14.refs_2_, ...), custom_call_target="tpu_custom_call" | custom-call | tf_op jit(solution)/shard_map/pallas_call | solution.py:623

commit v4 on v3

--- a/solution.py
+++ b/solution.py
@@ -610,22 +610,29 @@
 
 
 def settle_kernel(*refs):
-    n = len(refs) // 2
-    copies = [pltpu.make_async_copy(refs[i], refs[n + i], refs[-1].at[i]) for i in range(n)]
-    for copy in copies:
+    n = (len(refs) - 2) // 3
+    given, taken, held, come, gone = refs[:n], refs[n : 2 * n], refs[2 * n : 3 * n], refs[-2], refs[-1]
+    reads = [pltpu.make_async_copy(given[i], held[i], come.at[i]) for i in range(n)]
+    writes = [pltpu.make_async_copy(held[i], taken[i], gone.at[i]) for i in range(n)]
+    for copy in reads:
         copy.start()
-    for copy in copies:
+    for i in range(n):
+        reads[i].wait()
+        writes[i].start()
+    for copy in writes:
         copy.wait()
 
 
 def settle(*arrays):
     anywhere = pl.BlockSpec(memory_space=pl.ANY)
+    n = len(arrays)
     return pl.pallas_call(
         settle_kernel,
         out_shape=tuple(jax.ShapeDtypeStruct(a.shape, a.dtype) for a in arrays),
-        in_specs=[anywhere] * len(arrays),
-        out_specs=(anywhere,) * len(arrays),
-        scratch_shapes=[pltpu.SemaphoreType.DMA((len(arrays),))],
+        in_specs=[anywhere] * n,
+        out_specs=(anywhere,) * n,
+        scratch_shapes=[pltpu.VMEM(a.shape, a.dtype) for a in arrays] + [pltpu.SemaphoreType.DMA((n,))] * 2,
+        compiler_params=pltpu.CompilerParams(vmem_limit_bytes=VMEM_LIMIT),
     )(*arrays)
 
 

time: 185 us -> 114 us (0.62)
  Pallas kernels: 184 us -> 113 us
    pallas_call x1, Pallas kernels: 73.6 us -> 2.7 us  [settle(): pl.pallas_call(settle_kernel, out_shape=tuple((jax.ShapeDtypeStruct(a.sha...]
where the time goes in v4:
time: 114 us
  Pallas kernels  113 us (99%)
    pallas_call x1, Pallas kernels, update(): pl.pallas_call(update_kernel, out_shape=(jax.ShapeDtypeStruct((rows, 1024...  110 us
    pallas_call x1, Pallas kernels, settle(): pl.pallas_call(settle_kernel, out_shape=tuple((jax.ShapeDtypeStruct(a.sha...  2.7 us

profile of v4, /device:TPU:8, one launch (start us, length us, event | category | flops | bytes accessed | tf_op | source)
XLA Modules:
  0.0 113.5 jit_solution(3941085061432895156)
XLA Ops:
  0.6 110.2 %shard_map.93 = (bf16[128,1024]{1,0:T(8,128)(2,1)}, bf16[128,4096]{1,0:T(8,128)(2,1)}, f32[512,512]{1,0:T(8,128)}, bf16[128,128]{1,0:T(8,128)(2,1)}) custom-call(s32[16]{0:T(128)} %table.1, bf16[128,4096]{1,0:T(8,128)(2,1)} %tok.1, bf16[128,1024]{1,0:T(8,128)(2,1)} %ups.1, bf16[128,1024]{1,0:T(8,128)(2,1)} %shard.1, f32[512,512]{1,0:T(8,128)} %bitcast.3, ...), custom_call_target="tpu_custom_call" | custom-call | bytes 67108864 | tf_op jit(solution)/shard_map/pallas_call | solution.py:555
  110.8 2.7 %shard_map.94 = (bf16[128,1024]{1,0:T(8,128)(2,1)}, bf16[128,4096]{1,0:T(8,128)(2,1)}, f32[512,512]{1,0:T(8,128)}, bf16[128,128]{1,0:T(8,128)(2,1)}) custom-call(bf16[128,1024]{1,0:T(8,128)(2,1)} %get-tuple-element.12.refs_0_, bf16[128,4096]{1,0:T(8,128)(2,1)} %get-tuple-element.13.refs_1_, f32[512,512]{1,0:T(8,128)} %get-tuple-element.14.refs_2_, ...), custom_call_target="tpu_custom_call" | custom-call | tf_op jit(solution)/shard_map/pallas_call | solution.py:629

commit v5 on v4

v5 whole, which is shorter than its diff:
```python
import jax
import jax.numpy as jnp
from jax import lax
from jax.experimental import pallas as pl
from jax.experimental.pallas import tpu as pltpu
from jax.sharding import PartitionSpec as P

STAT_DECAY = 0.8
NORM_EPSILON = 1e-06
MESH = pl.DeviceIdType.MESH
VMEM_LIMIT = 60 * 1024 * 1024

NX, NY, NZ = 4, 4, 8
BS = 512
ROWS = 128
COLS = 256
HALF = 64
NB = 16
RA = 48
WA = 768


def remote(src, dst, send, recv, dp, fsdp):
    return pltpu.make_async_remote_copy(
        src_ref=src,
        dst_ref=dst,
        send_sem=send,
        recv_sem=recv,
        device_id=(dp, fsdp),
        device_id_type=MESH,
    )


def lanes(start, size):
    return pl.ds(pl.multiple_of(start, 128), size)


def dot3(left, right, contract=((1,), (0,))):
    def split(a):
        high = a.astype(jnp.bfloat16)
        return high, (a - high.astype(jnp.float32)).astype(jnp.bfloat16)

    def one(a, b):
        return lax.dot_general(a, b, (contract, ((), ())), preferred_element_type=jnp.float32)

    (lh, ll), (rh, rl) = split(left), split(right)
    return one(lh, rh) + (one(lh, rl) + one(ll, rh))


def update_kernel(
    table, tok, ups, shard, stats_prev, root_prev,
    projected, input_grad, root, out,
    block, weight, tok_own, ups_own, stats, start, square, fourth, moment, factor, iterate,
    projected_sum, rows_out, rows_in, energies, norms, chunks, spread, picked, raw,
    tok_in, tok_t, ups_in, part, outgoing, xa_in, za_sum, za_in, zb_in, xb_sum, xb_in,
    t_send, t_recv, f_send, f_recv, u_send, u_recv,
    xa_send, xa_recv, za_send, za_recv, zb_send, zb_recv, xb_send, xb_recv,
    g_send, g_recv, h_send, h_recv,
    wza_send, wza_recv, wxa_send, wxa_recv, wzb_send, wzb_recv, wxb_send, wxb_recv,
    wy_send, wy_recv, wf_send, wf_recv, wc_send, wc_recv, own,
    a_send, a_recv, e_send, e_recv, n_send, n_recv, s_send, s_recv, p_send, p_recv,
):
    me, fs = lax.axis_index("dp"), lax.axis_index("fsdp")
    y, core, x, z = me // 2, me % 2, fs // 8, fs % 8
    side = z % 2
    sibling = y * 2 + 1 - core
    mate = x * 8 + z + 1 - 2 * side

    def to_x(d):
        return lax.rem(x + d, 4)

    def to_y(d):
        return lax.rem(y + d, 4)

    def to_z(d):
        return lax.rem(z + d, 8)

    peers = [(me, x * 8 + to_z(d)) for d in (4, 3, 5, 2, 6, 1, 7)]
    peers += [(me, to_x(d) * 8 + z) for d in (2, 1, 3)]
    peers += [(lax.rem(me + d, 8), fs) for d in range(1, 8)]

    group, piece = fs // 2, z % 4
    sources = [(2 * piece + i, 2 * (4 * q + me % 4) + 1, i, q) for i in range(2) for q in range(4)]
    my_quarter, my_cols = group // 4, group % 4
    places = [
        (4 * b + my_cols, 4 * r + me // 2, 2 * r + b) for r in range(8) for b in range(2)
    ]

    def away(dp, fsdp):
        return jnp.logical_or(dp != me, fsdp != fs)

    barrier = pltpu.get_barrier_semaphore()

    def tell(dp, fsdp):
        pl.semaphore_signal(barrier, inc=1, device_id=(dp, fsdp), device_id_type=MESH)

    for dp, fsdp in peers:
        tell(dp, fsdp)

    local = [
        pltpu.make_async_copy(root_prev, start, own.at[3]),
        pltpu.make_async_copy(stats_prev, stats, own.at[4]),
        pltpu.make_async_copy(tok, tok_own, own.at[5]),
        pltpu.make_async_copy(ups, ups_own, own.at[6]),
    ]
    for copy in local:
        copy.start()

    pl.semaphore_wait(barrier, len(peers))

    def token_parts(of_y, where):
        for r in range(8):
            yield tok.at[:, lanes(512 * r + 128 * of_y, 128)], where.at[me, :, pl.ds(128 * r, 128)]

    def upstream_parts(of_core, half):
        for b in range(2):
            yield (
                ups.at[:, lanes(512 * b + 256 * of_core + 128 * half, 128)],
                ups_in.at[half, me, :, pl.ds(128 * b, 128)],
            )

    for d in (2, 1, 3):
        for src, dst in token_parts(to_y(d), tok_in):
            remote(src, dst, t_send.at[d], t_recv.at[d], to_y(d) * 2 + core, fs).start()
    for src, dst in token_parts(y, tok_in):
        remote(src, dst, f_send.at[0], f_recv.at[0], sibling, fs).start()

    def rows_of(of_y, of_core):
        return pl.ds(pl.multiple_of(32 * of_y + 16 * of_core, 16), 16)

    own_rows = rows_of(y, core)
    ca, cb = pl.ds(0, WA), pl.ds(WA, 1024 - WA)

    def wza(d):
        return remote(
            shard.at[own_rows, ca], weight.at[x, z, own_rows, ca],
            wza_send.at[d], wza_recv.at[d], me, x * 8 + to_z(d),
        )

    def wxb(d):
        return remote(
            shard.at[own_rows, cb], weight.at[x, z, own_rows, cb],
            wxb_send.at[d], wxb_recv.at[d], me, to_x(d) * 8 + z,
        )

    def wxa(d):
        slab = weight.at[x, :, own_rows, ca]
        return remote(slab, slab, wxa_send.at[d], wxa_recv.at[d], me, to_x(d) * 8 + z)

    def wzb(d):
        slab = weight.at[:, z, own_rows, cb]
        return remote(slab, slab, wzb_send.at[d], wzb_recv.at[d], me, x * 8 + to_z(d))

    def wza_in(d):
        spot = weight.at[x, lax.rem(z + 8 - d, 8), own_rows, ca]
        return remote(spot, spot, wza_send.at[d], wza_recv.at[d], me, mate)

    def wxb_in(d):
        spot = weight.at[lax.rem(x + 4 - d, 4), z, own_rows, cb]
        return remote(spot, spot, wxb_send.at[d], wxb_recv.at[d], me, mate)

    def wxa_in(d):
        spot = weight.at[lax.rem(x + 4 - d, 4), :, own_rows, ca]
        return remote(spot, spot, wxa_send.at[d], wxa_recv.at[d], me, mate)

    def wzb_in(d):
        spot = weight.at[:, lax.rem(z + 8 - d, 8), own_rows, cb]
        return remote(spot, spot, wzb_send.at[d], wzb_recv.at[d], me, mate)

    own_shard = pltpu.make_async_copy(shard.at[own_rows], weight.at[x, z, own_rows], own.at[8])
    own_shard.start()
    for d in (4, 3, 5, 2, 6, 1, 7):
        wza(d).start()
    for d in (2, 1, 3):
        wxb(d).start()

    for half in range(2):
        for d in (2, 1, 3, 0):
            for flip in range(2):
                if d == 0 and flip == 0:
                    continue
                of_core = core if flip == 0 else 1 - core
                for src, dst in upstream_parts(of_core, half):
                    k = 2 * d + flip
                    remote(
                        src, dst, u_send.at[half, k], u_recv.at[half, k], to_y(d) * 2 + of_core, fs
                    ).start()
    for src, dst in token_parts(y, tok_in):
        pltpu.make_async_copy(src, dst, own.at[0]).start()
    for half in range(2):
        for src, dst in upstream_parts(core, half):
            pltpu.make_async_copy(src, dst, own.at[half + 1]).start()

    def whole(send, recv, slot):
        return remote(tok_in.at[slot], tok_in.at[slot], send, recv, sibling, fs)

    def turn(slot):
        tok_t[:, lanes(slot * 128, 128)] = tok_in[slot].T

    pltpu.make_async_copy(tok_in.at[me], tok_in.at[me], own.at[0]).wait()
    turn(me)
    whole(f_send.at[0], f_recv.at[0], sibling).wait_recv()
    turn(sibling)

    local[0].wait()
    square[...] = dot3(start[...], start[...])

    own_shard.wait()
    for d in (1, 3, 2):
        wxb_in(d).wait_recv()
    for d in (1, 7, 2, 6, 3, 5, 4):
        wza_in(d).wait_recv()
    for d in (2, 1, 3):
        wxa(d).start()
    for d in (4, 3, 5, 2, 6, 1, 7):
        wzb(d).start()

    fourth[...] = dot3(square[...], square[...])

    for d in (1, 3, 2):
        slot = lax.rem(y + 4 - d, 4) * 2 + core
        whole(t_send.at[d], t_recv.at[d], slot).wait_recv()
        whole(f_send.at[d], f_recv.at[d], slot).start()
        turn(slot)
    for d in (1, 3, 2):
        slot = lax.rem(y + 4 - d, 4) * 2 + 1 - core
        whole(f_send.at[d], f_recv.at[d], slot).wait_recv()
        turn(slot)
    def upstream_arrived(half):
        for d in (0, 1, 3, 2):
            for flip in range(2):
                if d == 0 and flip == 0:
                    continue
                from_core = core if flip == 0 else 1 - core
                spot = ups_in.at[half, lax.rem(y + 4 - d, 4) * 2 + from_core]
                k = 2 * d + flip
                remote(spot, spot, u_send.at[half, k], u_recv.at[half, k], sibling, fs).wait()
        pltpu.make_async_copy(ups_in.at[half, me], ups_in.at[half, me], own.at[half + 1]).wait()

    def multiply(half):
        def body(i, _):
            rows = tok_t[pl.ds(pl.multiple_of(i * 256, 256), 256), :]
            piece = jnp.dot(
                rows, ups_in[half].reshape(1024, COLS), preferred_element_type=jnp.float32
            )
            part[half, 2 * i] = piece[:ROWS]
            part[half, 2 * i + 1] = piece[ROWS:]
            return 0

        lax.fori_loop(0, 4, body, 0)

    def arrange(half, of_x):
        def body(i, _):
            chosen = table[of_x * 4 + i]
            both = part[half, lax.div(chosen, 2)]
            piece = jnp.where(lax.rem(chosen, 2) == 0, both[:, :128], both[:, 128:])
            outgoing[half, of_x, 2 * i] = piece[:HALF]
            outgoing[half, of_x, 2 * i + 1] = piece[HALF:]
            return 0

        lax.fori_loop(0, 4, body, 0)

    rows_a, rows_b = pl.ds(0, RA), pl.ds(RA, HALF - RA)

    def xa(h, d):
        return remote(
            outgoing.at[h, to_x(d), :, rows_a], xa_in.at[h, d],
            xa_send.at[h, d], xa_recv.at[h, d], me, to_x(d) * 8 + z,
        )

    def zb(h, d):
        return remote(
            outgoing.at[h, :, to_z(d), rows_b], zb_in.at[h, d],
            zb_send.at[h, d], zb_recv.at[h, d], me, x * 8 + to_z(d),
        )

    def za(h, d):
        return remote(
            za_sum.at[h, to_z(d)], za_in.at[h, d], za_send.at[h, d], za_recv.at[h, d], me, x * 8 + to_z(d)
        )

    def xb(h, d):
        return remote(
            xb_sum.at[h, to_x(d)], xb_in.at[h, d], xb_send.at[h, d], xb_recv.at[h, d], me, to_x(d) * 8 + z
        )

    def first_sums(h):
        for d in (1, 7, 2, 6, 3, 5, 4):
            zb(h, d).wait_recv()
        for d in (2, 1, 3, 0):
            to = to_x(d)
            total = outgoing[h, to, z, RA:]
            for k in range(1, 8):
                total = total + zb_in[h, k, to]
            xb_sum[h, to] = total
            if d:
                xb(h, d).start()
        for d in (1, 3, 2):
            xa(h, d).wait_recv()
        for d in (4, 3, 5, 2, 6, 1, 7, 0):
            to = to_z(d)
            za_sum[h, to] = (outgoing[h, x, to, :RA] + xa_in[h, 1, to]) + (xa_in[h, 2, to] + xa_in[h, 3, to])
            if d:
                za(h, d).start()

    for h in range(2):
        upstream_arrived(h)
        multiply(h)
        for d in (2, 1, 3, 0):
            arrange(h, to_x(d))
            if d:
                xa(h, d).start()
        for d in (4, 3, 5, 2, 6, 1, 7):
            zb(h, d).start()

    for d in (1, 3, 2):
        wxa_in(d).wait_recv()
    for d in (1, 7, 2, 6, 3, 5, 4):
        wzb_in(d).wait_recv()

    def wy(d, spot):
        return remote(spot, spot, wy_send.at[d], wy_recv.at[d], to_y(d) * 2 + core, fs)

    def wf(d, spot):
        return remote(spot, spot, wf_send.at[d], wf_recv.at[d], to_y(d) * 2 + core, fs)

    def wc(k, spot):
        return remote(spot, spot, wc_send.at[k], wc_recv.at[k], sibling, fs)

    def rows_from(d, of_core):
        return weight.at[:, :, rows_of(lax.rem(y + 4 - d, 4), of_core)]

    def half_from(d, of_y):
        return weight.at[pl.ds(0 if d == 1 else 2, 2), :, rows_of(of_y, core)]

    wy(1, rows_from(0, core)).start()
    wy(3, rows_from(0, core)).start()
    wc(0, rows_from(0, core)).start()

    first_sums(0)

    first_sums(1)

    def place(h, of_y, of_side, of_core):
        return block.at[
            pl.ds(pl.multiple_of(of_y * ROWS + of_side * HALF, HALF), HALF),
            lanes(of_core * COLS + h * 128, 128),
        ]

    def mine(h):
        return place(h, y, side, core)

    def g_copy(h, d, flip, spot):
        k = 2 * d + flip
        return remote(
            spot, spot, g_send.at[h, k], g_recv.at[h, k], to_y(d) * 2 + core, mate if flip else fs
        )

    def h_copy(h, k, spot):
        return remote(spot, spot, h_send.at[h, k], h_recv.at[h, k], sibling, fs)

    order = [(d, flip) for d in (2, 1, 3, 0) for flip in range(2) if d or flip]
    for h in range(2):
        total = xb_sum[h, x]
        for d in (1, 3, 2):
            xb(h, d).wait_recv()
            total = total + xb_in[h, d]
        mine(h)[rows_b] = total
        total = za_sum[h, z]
        for d in (1, 7, 2, 6, 3, 5, 4):
            za(h, d).wait_recv()
            total = total + za_in[h, d]
        mine(h)[rows_a] = total
        for d, flip in order:
            g_copy(h, d, flip, mine(h)).start()
        h_copy(h, 0, mine(h)).start()

    for h in range(2):
        for d, flip in reversed(order):
            spot = place(h, lax.rem(y + 4 - d, 4), 1 - side if flip else side, core)
            g_copy(h, d, flip, spot).wait_recv()
            h_copy(h, 2 * d + flip, spot).start()

    for h in range(2):
        for d in range(4):
            for flip in range(2):
                spot = place(h, lax.rem(y + 4 - d, 4), 1 - side if flip else side, 1 - core)
                h_copy(h, 2 * d + flip, spot).wait()

    for d in (1, 3):
        wy(d, rows_from(d, core)).wait_recv()
        wf(d, half_from(d, lax.rem(y + 4 - d, 4))).start()
        wc(d, rows_from(d, core)).start()

    local[1].wait()

    @pl.when(side == 0)
    def _():
        moment[...] = dot3(block[...], block[...], ((1,), (1,)))

    @pl.when(side == 1)
    def _():
        moment[...] = dot3(block[...], block[...], ((0,), (0,)))

    diagonal = lax.broadcasted_iota(jnp.int32, (BS, BS), 0) == lax.broadcasted_iota(jnp.int32, (BS, BS), 1)
    fresh = STAT_DECAY * stats[...] + (1.0 - STAT_DECAY) * moment[...]
    trace = jnp.sum(jnp.where(diagonal, fresh, 0.0))
    stats[...] = fresh / (trace / BS)

    def next_factor():
        return (jnp.where(diagonal, 5.0, 0.0) - moment[...]) * 0.25

    moment[...] = dot3(fourth[...], stats[...])
    factor[...] = next_factor()
    square[...] = dot3(factor[...], factor[...])
    fourth[...] = dot3(square[...], square[...])
    iterate[...] = dot3(start[...], factor[...])
    moment[...] = dot3(fourth[...], moment[...])
    factor[...] = next_factor()

    def a_copy():
        return remote(rows_out, rows_in, a_send, a_recv, me, mate)

    @pl.when(side == 0)
    def _():
        mine_rows = iterate[pl.ds(pl.multiple_of(me * HALF, HALF), HALF), :]
        rows_out[...] = dot3(dot3(mine_rows, factor[...]), block[...])
        a_copy().start()

    root[...] = dot3(iterate[...], factor[...])


    local[2].wait()
    local[3].wait()

    def products(i):
        band = weight[i].reshape(1024, 1024)
        here = jnp.dot(tok_own[:, 1024 * i : 1024 * i + 1024], band, preferred_element_type=jnp.float32)
        if i:
            here = here + projected_sum[...]
        if i < 3:
            projected_sum[...] = here
        else:
            projected[...] = here.astype(jnp.bfloat16)
        input_grad[:, 1024 * i : 1024 * i + 1024] = lax.dot_general(
            ups_own[...], band, (((1,), (1,)), ((), ())), preferred_element_type=jnp.float32
        ).astype(jnp.bfloat16)

    def e_copy(d):
        return remote(energies.at[0], energies.at[d], e_send.at[d], e_recv.at[d], lax.rem(me + d, 8), fs)

    def s_copy(d):
        to = lax.rem(group + d, NB)
        return remote(chunks.at[to], spread.at[group], s_send.at[d], s_recv.at[d], me, 2 * to + 1)

    def n_copy(d):
        return remote(
            norms.at[group], norms.at[group], n_send.at[d], n_recv.at[group], me, lax.rem(fs + d, 32)
        )

    def out_rows(i, q):
        return raw.at[pl.ds(pl.multiple_of(HALF * i + 16 * q, 16), 16)]

    def p_copy(dp, fsdp, b):
        return remote(
            picked.at[b], out_rows(me % 2, my_quarter), p_send.at[b],
            p_recv.at[4 * (me % 2) + my_quarter], dp, fsdp,
        )

    def holder_of(b):
        holder = jnp.int32(0)
        for g in range(1, NB):
            holder = jnp.maximum(holder, jnp.where(table[g] == b, g, 0))
        return holder

    def p_home(b):
        return pltpu.make_async_copy(picked.at[b], out_rows(me % 2, my_quarter), own.at[7])

    @pl.when(side == 1)
    def _():
        a_copy().wait_recv()
        product = dot3(rows_in[...], root[...])
        energies[0] = jnp.full((8, 128), jnp.sum(product * product), jnp.float32)
        for d in (4, 5, 2, 3, 6, 7, 1):
            e_copy(d).start()
        for j in range(NB):
            q, c = j // 4, j % 4
            chunks[j] = product[16 * q : 16 * q + 16, 128 * c : 128 * c + 128]
        for d in (8, 7, 9, 6, 10, 5, 11, 4, 12, 3, 13, 2, 14, 1, 15):
            s_copy(d).start()
        spread[group] = chunks[group]
        for d in range(1, 8):
            e_copy(d).wait_recv()
        total = jnp.zeros((8, 128), jnp.float32)
        for dp in range(8):
            total = total + energies[lax.rem(me - dp + 8, 8)]
        norms[group] = total
        for d in range(1, 32):
            n_copy(d).start()

    for d in (1, 3):
        wf(d, half_from(d, to_y(2))).wait_recv()
    wc(2, rows_from(2, core)).start()
    for d in (0, 1, 3, 2):
        wc(d, rows_from(d, 1 - core)).wait()

    products(0)
    products(1)
    products(2)

    @pl.when(side == 1)
    def _():
        for d in range(1, NB):
            source = lax.rem(group + NB - d, NB)
            remote(
                chunks.at[0], spread.at[source], s_send.at[d], s_recv.at[d], me, 2 * source + 1
            ).wait_recv()
        for dp, fsdp, b in places:
            picked[b] = spread[holder_of(b)]

            @pl.when(away(dp, fsdp))
            def _(dp=dp, fsdp=fsdp, b=b):
                p_copy(dp, fsdp, b).start()

            @pl.when(jnp.logical_not(away(dp, fsdp)))
            def _(b=b):
                p_home(b).start()

    products(3)

    for dp, fsdp, i, q in sources:
        @pl.when(away(dp, fsdp))
        def _(dp=dp, fsdp=fsdp, i=i, q=q):
            remote(picked.at[0], out_rows(i, q), p_send.at[0], p_recv.at[4 * i + q], dp, fsdp).wait_recv()

    for g in range(NB):
        @pl.when(fs != 2 * g + 1)
        def _(g=g):
            remote(norms.at[g], norms.at[g], n_send.at[1], n_recv.at[g], me, mate).wait_recv()

    @pl.when(side == 1)
    def _():
        for dp, fsdp, b in places:
            @pl.when(jnp.logical_not(away(dp, fsdp)))
            def _(b=b):
                p_home(b).wait()

    here = 2 * (fs // 4) + me // 4
    mean = norms[holder_of(here)][0:1, 0:1] / (BS * BS)
    out[...] = (raw[...] / jnp.sqrt(mean + NORM_EPSILON)).astype(jnp.bfloat16)

    @pl.when(side == 0)
    def _():
        a_copy().wait_send()

    @pl.when(side == 1)
    def _():
        for d in range(1, 8):
            e_copy(d).wait_send()
        for d in range(1, NB):
            s_copy(d).wait_send()
        for dp, fsdp, b in places:
            @pl.when(away(dp, fsdp))
            def _(dp=dp, fsdp=fsdp, b=b):
                p_copy(dp, fsdp, b).wait_send()
        for d in range(1, 32):
            n_copy(d).wait_send()

    for d in range(1, 4):
        whole(t_send.at[d], t_recv.at[d], me).wait_send()
        wxa(d).wait_send()
        wxb(d).wait_send()
    for d in range(4):
        whole(f_send.at[d], f_recv.at[d], me).wait_send()
    for d in range(1, 8):
        wza(d).wait_send()
        wzb(d).wait_send()
    for h in range(2):
        for d in range(1, 4):
            xa(h, d).wait_send()
            xb(h, d).wait_send()
        for d in range(1, 8):
            za(h, d).wait_send()
            zb(h, d).wait_send()
        for d, flip in order:
            g_copy(h, d, flip, mine(h)).wait_send()
    for d in (1, 3):
        wy(d, rows_from(0, core)).wait_send()
        wf(d, half_from(d, y)).wait_send()


def update(table, tokens, upstream, shard, stats_prev, root_prev):
    dma = pltpu.SemaphoreType.DMA
    f32, b16 = jnp.float32, jnp.bfloat16
    anywhere, vmem = pl.BlockSpec(memory_space=pl.ANY), pl.BlockSpec(memory_space=pltpu.VMEM)
    rows = tokens.shape[0]
    square = pltpu.VMEM((BS, BS), f32)
    return pl.pallas_call(
        update_kernel,
        out_shape=(
            jax.ShapeDtypeStruct((rows, 1024), b16),
            jax.ShapeDtypeStruct((rows, 4096), b16),
            jax.ShapeDtypeStruct((BS, BS), f32),
            jax.ShapeDtypeStruct((128, 128), b16),
        ),
        in_specs=[pl.BlockSpec(memory_space=pltpu.SMEM)] + [anywhere] * 5,
        out_specs=(vmem,) * 4,
        scratch_shapes=[
            square,
            pltpu.VMEM((NX, NZ, 128, 1024), b16),
            pltpu.VMEM((rows, 4096), b16),
            pltpu.VMEM((rows, 1024), b16),
        ]
        + [square] * 7
        + [
            pltpu.VMEM((rows, 1024), f32),
            pltpu.VMEM((HALF, BS), f32),
            pltpu.VMEM((HALF, BS), f32),
            pltpu.VMEM((8, 8, 128), f32),
            pltpu.VMEM((NB, 8, 128), f32),
            pltpu.VMEM((NB, 16, 128), f32),
            pltpu.VMEM((NB, 16, 128), f32),
            pltpu.VMEM((NB, 16, 128), f32),
            pltpu.VMEM((128, 128), f32),
            pltpu.VMEM((8, rows, 1024), b16),
            pltpu.VMEM((1024, 8 * rows), b16),
            pltpu.VMEM((2, 8, rows, COLS), b16),
            pltpu.VMEM((2, 8, ROWS, COLS), f32),
            pltpu.VMEM((2, NX, NZ, HALF, 128), f32),
            pltpu.VMEM((2, NX, NZ, RA, 128), f32),
            pltpu.VMEM((2, NZ, RA, 128), f32),
            pltpu.VMEM((2, NZ, RA, 128), f32),
            pltpu.VMEM((2, NZ, NX, HALF - RA, 128), f32),
            pltpu.VMEM((2, NX, HALF - RA, 128), f32),
            pltpu.VMEM((2, NX, HALF - RA, 128), f32),
        ]
        + [dma((4,))] * 4
        + [dma((2, 8))] * 2
        + [dma((2, 4))] * 2
        + [dma((2, 8))] * 4
        + [dma((2, 4))] * 2
        + [dma((2, 8))] * 4
        + [dma((8,))] * 2
        + [dma((4,))] * 2
        + [dma((8,))] * 2
        + [dma((4,))] * 8
        + [dma((9,)), dma(()), dma(()), dma((8,)), dma((8,)), dma((32,)), dma((NB,))]
        + [dma((NB,))] * 3
        + [dma((8,))],
        compiler_params=pltpu.CompilerParams(
            collective_id=0, has_side_effects=True, vmem_limit_bytes=VMEM_LIMIT
        ),
        cost_estimate=pl.CostEstimate(flops=0, bytes_accessed=64 << 20, transcendentals=0),
    )(table, tokens, upstream, shard, stats_prev, root_prev)


def settle_kernel(*refs):
    n = (len(refs) - 2) // 3
    given, taken, held, come, gone = refs[:n], refs[n : 2 * n], refs[2 * n : 3 * n], refs[-2], refs[-1]
    reads = [pltpu.make_async_copy(given[i], held[i], come.at[i]) for i in range(n)]
    writes = [pltpu.make_async_copy(held[i], taken[i], gone.at[i]) for i in range(n)]
    for copy in reads:
        copy.start()
    for i in range(n):
        reads[i].wait()
        writes[i].start()
    for copy in writes:
        copy.wait()


def settle(*arrays):
    anywhere = pl.BlockSpec(memory_space=pl.ANY)
    n = len(arrays)
    return pl.pallas_call(
        settle_kernel,
        out_shape=tuple(jax.ShapeDtypeStruct(a.shape, a.dtype) for a in arrays),
        in_specs=[anywhere] * n,
        out_specs=(anywhere,) * n,
        scratch_shapes=[pltpu.VMEM(a.shape, a.dtype) for a in arrays] + [pltpu.SemaphoreType.DMA((n,))] * 2,
        compiler_params=pltpu.CompilerParams(vmem_limit_bytes=VMEM_LIMIT),
    )(*arrays)


def local(tokens, upstream, weight, owner_table, stats_prev, roots_prev):
    projected, input_grad, root, direction = settle(
        *update(owner_table, tokens, upstream, weight, stats_prev[0], roots_prev[0])
    )
    return projected, input_grad, root[None], direction


def solution(mesh):
    placed = (
        P(("dp", "fsdp"), None),
        P(("dp", "fsdp"), None),
        P("fsdp", None),
        P(),
        P("fsdp", None, None),
        P("fsdp", None, None),
    )
    return jax.shard_map(
        local,
        mesh=mesh,
        in_specs=placed,
        out_specs=(
            P(("dp", "fsdp"), None),
            P(("dp", "fsdp"), None),
            P("fsdp", None, None),
            P("fsdp", "dp"),
        ),
        check_vma=False,
    )
```

time: 114 us -> 106 us (0.930)
  Pallas kernels: 113 us -> 104 us
    pallas_call x1, Pallas kernels: 110 us -> 101 us  [update(): pl.pallas_call(update_kernel, out_shape=(jax.ShapeDtypeStruct((rows, 1024...]
where the time goes in v5:
time: 106 us; the launch traced here: 105 us
  Pallas kernels  104 us (98%)
    pallas_call x1, Pallas kernels, update(): pl.pallas_call(update_kernel, out_shape=(jax.ShapeDtypeStruct((rows, 1024...  101 us
    pallas_call x1, Pallas kernels, settle(): pl.pallas_call(settle_kernel, out_shape=tuple((jax.ShapeDtypeStruct(a.sha...  2.7 us

profile of v5, /device:TPU:8, one launch (start us, length us, event | category | flops | bytes accessed | tf_op | source)
XLA Modules:
  0.0 104.5 jit_solution(933234610390176625)
XLA Ops:
  0.6 101.0 %shard_map.93 = (bf16[128,1024]{1,0:T(8,128)(2,1)}, bf16[128,4096]{1,0:T(8,128)(2,1)}, f32[512,512]{1,0:T(8,128)}, bf16[128,128]{1,0:T(8,128)(2,1)}) custom-call(s32[16]{0:T(128)} %table.1, bf16[128,4096]{1,0:T(8,128)(2,1)} %tok.1, bf16[128,1024]{1,0:T(8,128)(2,1)} %ups.1, bf16[128,1024]{1,0:T(8,128)(2,1)} %shard.1, f32[512,512]{1,0:T(8,128)} %bitcast.3, ...), custom_call_target="tpu_custom_call" | custom-call | bytes 67108864 | tf_op jit(solution)/shard_map/pallas_call | solution.py:598
  101.7 2.7 %shard_map.94 = (bf16[128,1024]{1,0:T(8,128)(2,1)}, bf16[128,4096]{1,0:T(8,128)(2,1)}, f32[512,512]{1,0:T(8,128)}, bf16[128,128]{1,0:T(8,128)(2,1)}) custom-call(bf16[128,1024]{1,0:T(8,128)(2,1)} %get-tuple-element.12.refs_0_, bf16[128,4096]{1,0:T(8,128)(2,1)} %get-tuple-element.13.refs_1_, f32[512,512]{1,0:T(8,128)} %get-tuple-element.14.refs_2_, ...), custom_call_target="tpu_custom_call" | custom-call | tf_op jit(solution)/shard_map/pallas_call | solution.py:674

commit v6 on v5

--- a/solution.py
+++ b/solution.py
@@ -52,9 +52,9 @@
     projected, input_grad, root, out,
     block, weight, tok_own, ups_own, stats, start, square, fourth, moment, factor, iterate,
     projected_sum, rows_out, rows_in, energies, norms, chunks, spread, picked, raw,
-    tok_in, tok_t, ups_in, part, outgoing, xa_in, za_sum, za_in, zb_in, xb_sum, xb_in,
+    tok_in, tok_t, ups_in, part, outgoing, xr_in, xr_sum, xa_in, za_sum, za_in, zb_in, xb_sum, xb_in,
     t_send, t_recv, f_send, f_recv, u_send, u_recv,
-    xa_send, xa_recv, za_send, za_recv, zb_send, zb_recv, xb_send, xb_recv,
+    xr_send, xr_recv, xd_send, xd_recv, xa_send, xa_recv, za_send, za_recv, zb_send, zb_recv, xb_send, xb_recv,
     g_send, g_recv, h_send, h_recv,
     wza_send, wza_recv, wxa_send, wxa_recv, wzb_send, wzb_recv, wxb_send, wxb_recv,
     wy_send, wy_recv, wf_send, wf_recv, wc_send, wc_recv, own,
@@ -262,11 +262,26 @@
 
     rows_a, rows_b = pl.ds(0, RA), pl.ds(RA, HALF - RA)
 
-    def xa(h, d):
-        return remote(
-            outgoing.at[h, to_x(d), :, rows_a], xa_in.at[h, d],
-            xa_send.at[h, d], xa_recv.at[h, d], me, to_x(d) * 8 + z,
-        )
+    low, high = pl.ds(0, 4), pl.ds(4, 4)
+
+    def xr(h, i):
+        src = outgoing.at[h, to_x(2), (low, high)[i], rows_a]
+        return remote(src, xr_in.at[h, i], xr_send.at[h, i], xr_recv.at[h, i], me, to_x((1, 3)[i]) * 8 + z)
+
+    def xd(h, i):
+        src = outgoing.at[h, to_x((1, 3)[i]), (high, low)[i], rows_a]
+        dst = xa_in.at[h, i, (high, low)[i]]
+        return remote(src, dst, xd_send.at[h, i], xd_recv.at[h, i], me, to_x((1, 3)[i]) * 8 + z)
+
+    def xa(h, i):
+        dst = xa_in.at[h, i, (low, high)[i]]
+        return remote(xr_sum.at[h, i], dst, xa_send.at[h, i], xa_recv.at[h, i], me, to_x((1, 3)[i]) * 8 + z)
+
+    def relay(h):
+        for i in range(2):
+            xr(h, i).wait_recv()
+            xr_sum[h, i] = xr_in[h, i] + outgoing[h, to_x((1, 3)[i]), (low, high)[i], rows_a]
+            xa(h, i).start()
 
     def zb(h, d):
         return remote(
@@ -295,50 +310,72 @@
             xb_sum[h, to] = total
             if d:
                 xb(h, d).start()
-        for d in (1, 3, 2):
-            xa(h, d).wait_recv()
+        for i in range(2):
+            xd(h, i).wait_recv()
+            xa(h, i).wait_recv()
         for d in (4, 3, 5, 2, 6, 1, 7, 0):
             to = to_z(d)
-            za_sum[h, to] = (outgoing[h, x, to, :RA] + xa_in[h, 1, to]) + (xa_in[h, 2, to] + xa_in[h, 3, to])
+            za_sum[h, to] = outgoing[h, x, to, :RA] + (xa_in[h, 0, to] + xa_in[h, 1, to])
             if d:
                 za(h, d).start()
 
+    def wy(d, late, of_y):
+        first, count = {(1, 0): (0, 3), (1, 1): (3, 1), (3, 0): (1, 3), (3, 1): (0, 1)}[d, late]
+        spot = weight.at[pl.ds(first, count), :, rows_of(of_y, core)]
+        return remote(spot, spot, wy_send.at[late, d], wy_recv.at[late, d], to_y(d) * 2 + core, fs)
+
+    def wy_from(d, late):
+        return wy(d, late, lax.rem(y + 4 - d, 4))
+
+    def late_part(d, of_core):
+        first = 3 if d == 1 else 0
+        return weight.at[pl.ds(first, 1), :, rows_of(lax.rem(y + 4 - d, 4), of_core)]
+
+    def early_part(d, of_core):
+        first = 0 if d == 1 else 1
+        return weight.at[pl.ds(first, 3), :, rows_of(lax.rem(y + 4 - d, 4), of_core)]
+
+    def wf(d, spot):
+        return remote(spot, spot, wf_send.at[d], wf_recv.at[d], to_y(d) * 2 + core, fs)
+
+    def wc(k, spot):
+        return remote(spot, spot, wc_send.at[k], wc_recv.at[k], sibling, fs)
+
+    def rows_from(d, of_core):
+        return weight.at[:, :, rows_of(lax.rem(y + 4 - d, 4), of_core)]
+
+    def half_from(d, of_y):
+        return weight.at[pl.ds(0 if d == 1 else 2, 2), :, rows_of(of_y, core)]
+
+    def share():
+        for d in (1, 3, 2):
+            wxa_in(d).wait_recv()
+        for d in (1, 7, 2, 6, 3, 5, 4):
+            wzb_in(d).wait_recv()
+
+        wy(1, 0, y).start()
+        wy(3, 0, y).start()
+        wc(0, rows_from(0, core)).start()
+
     for h in range(2):
         upstream_arrived(h)
+        if h:
+            share()
+            relay(0)
         multiply(h)
-        for d in (2, 1, 3, 0):
-            arrange(h, to_x(d))
-            if d:
-                xa(h, d).start()
+        arrange(h, to_x(2))
+        for i in range(2):
+            xr(h, i).start()
+        arrange(h, to_x(1))
+        arrange(h, to_x(3))
+        for i in range(2):
+            xd(h, i).start()
+        arrange(h, x)
         for d in (4, 3, 5, 2, 6, 1, 7):
             zb(h, d).start()
 
-    for d in (1, 3, 2):
-        wxa_in(d).wait_recv()
-    for d in (1, 7, 2, 6, 3, 5, 4):
-        wzb_in(d).wait_recv()
-
-    def wy(d, spot):
-        return remote(spot, spot, wy_send.at[d], wy_recv.at[d], to_y(d) * 2 + core, fs)
-
-    def wf(d, spot):
-        return remote(spot, spot, wf_send.at[d], wf_recv.at[d], to_y(d) * 2 + core, fs)
-
-    def wc(k, spot):
-        return remote(spot, spot, wc_send.at[k], wc_recv.at[k], sibling, fs)
-
-    def rows_from(d, of_core):
-        return weight.at[:, :, rows_of(lax.rem(y + 4 - d, 4), of_core)]
-
-    def half_from(d, of_y):
-        return weight.at[pl.ds(0 if d == 1 else 2, 2), :, rows_of(of_y, core)]
-
-    wy(1, rows_from(0, core)).start()
-    wy(3, rows_from(0, core)).start()
-    wc(0, rows_from(0, core)).start()
-
     first_sums(0)
-
+    relay(1)
     first_sums(1)
 
     def place(h, of_y, of_side, of_core):
@@ -388,9 +425,10 @@
                 h_copy(h, 2 * d + flip, spot).wait()
 
     for d in (1, 3):
-        wy(d, rows_from(d, core)).wait_recv()
+        wy_from(d, 0).wait_recv()
         wf(d, half_from(d, lax.rem(y + 4 - d, 4))).start()
-        wc(d, rows_from(d, core)).start()
+        wy(d, 1, y).start()
+        wc(d, early_part(d, core)).start()
 
     local[1].wait()
 
@@ -498,15 +536,13 @@
         for d in range(1, 32):
             n_copy(d).start()
 
+
+    for d in (1, 3):
+        wy_from(d, 1).wait_recv()
+        wc(d + 3, late_part(d, core)).start()
     for d in (1, 3):
         wf(d, half_from(d, to_y(2))).wait_recv()
     wc(2, rows_from(2, core)).start()
-    for d in (0, 1, 3, 2):
-        wc(d, rows_from(d, 1 - core)).wait()
-
-    products(0)
-    products(1)
-    products(2)
 
     @pl.when(side == 1)
     def _():
@@ -526,7 +562,14 @@
             def _(b=b):
                 p_home(b).start()
 
-    products(3)
+    wc(0, rows_from(0, 1 - core)).wait()
+    wc(2, rows_from(2, 1 - core)).wait()
+    for d in (1, 3):
+        wc(d, early_part(d, 1 - core)).wait()
+        wc(d + 3, late_part(d, 1 - core)).wait()
+
+    for i in range(4):
+        products(i)
 
     for dp, fsdp, i, q in sources:
         @pl.when(away(dp, fsdp))
@@ -576,8 +619,11 @@
         wza(d).wait_send()
         wzb(d).wait_send()
     for h in range(2):
+        for i in range(2):
+            xr(h, i).wait_send()
+            xd(h, i).wait_send()
+            xa(h, i).wait_send()
         for d in range(1, 4):
-            xa(h, d).wait_send()
             xb(h, d).wait_send()
         for d in range(1, 8):
             za(h, d).wait_send()
@@ -585,7 +631,8 @@
         for d, flip in order:
             g_copy(h, d, flip, mine(h)).wait_send()
     for d in (1, 3):
-        wy(d, rows_from(0, core)).wait_send()
+        wy(d, 0, y).wait_send()
+        wy(d, 1, y).wait_send()
         wf(d, half_from(d, y)).wait_send()
 
 
@@ -627,7 +674,9 @@
             pltpu.VMEM((2, 8, rows, COLS), b16),
             pltpu.VMEM((2, 8, ROWS, COLS), f32),
             pltpu.VMEM((2, NX, NZ, HALF, 128), f32),
-            pltpu.VMEM((2, NX, NZ, RA, 128), f32),
+            pltpu.VMEM((2, 2, 4, RA, 128), f32),
+            pltpu.VMEM((2, 2, 4, RA, 128), f32),
+            pltpu.VMEM((2, 2, NZ, RA, 128), f32),
             pltpu.VMEM((2, NZ, RA, 128), f32),
             pltpu.VMEM((2, NZ, RA, 128), f32),
             pltpu.VMEM((2, NZ, NX, HALF - RA, 128), f32),
@@ -636,14 +685,17 @@
         ]
         + [dma((4,))] * 4
         + [dma((2, 8))] * 2
-        + [dma((2, 4))] * 2
+        + [dma((2, 2))] * 6
         + [dma((2, 8))] * 4
         + [dma((2, 4))] * 2
         + [dma((2, 8))] * 4
         + [dma((8,))] * 2
         + [dma((4,))] * 2
         + [dma((8,))] * 2
-        + [dma((4,))] * 8
+        + [dma((4,))] * 2
+        + [dma((2, 4))] * 2
+        + [dma((4,))] * 2
+        + [dma((8,))] * 2
         + [dma((9,)), dma(()), dma(()), dma((8,)), dma((8,)), dma((32,)), dma((NB,))]
         + [dma((NB,))] * 3
         + [dma((8,))],

time: 106 us -> 98.7 us (0.931)
  Pallas kernels: 104 us -> 96 us
    pallas_call x1, Pallas kernels: 101 us -> 93.3 us  [update(): pl.pallas_call(update_kernel, out_shape=(jax.ShapeDtypeStruct((rows, 1024...]
where the time goes in v6:
time: 98.7 us; the launch traced here: 96.8 us
  Pallas kernels  96 us (97%)
    pallas_call x1, Pallas kernels, update(): pl.pallas_call(update_kernel, out_shape=(jax.ShapeDtypeStruct((rows, 1024...  93.3 us
    pallas_call x1, Pallas kernels, settle(): pl.pallas_call(settle_kernel, out_shape=tuple((jax.ShapeDtypeStruct(a.sha...  2.7 us

profile of v6, /device:TPU:8, one launch (start us, length us, event | category | flops | bytes accessed | tf_op | source)
XLA Modules:
  0.0 96.8 jit_solution(15173830985414246162)
XLA Ops:
  0.6 93.3 %shard_map.93 = (bf16[128,1024]{1,0:T(8,128)(2,1)}, bf16[128,4096]{1,0:T(8,128)(2,1)}, f32[512,512]{1,0:T(8,128)}, bf16[128,128]{1,0:T(8,128)(2,1)}) custom-call(s32[16]{0:T(128)} %table.1, bf16[128,4096]{1,0:T(8,128)(2,1)} %tok.1, bf16[128,1024]{1,0:T(8,128)(2,1)} %ups.1, bf16[128,1024]{1,0:T(8,128)(2,1)} %shard.1, f32[512,512]{1,0:T(8,128)} %bitcast.3, ...), custom_call_target="tpu_custom_call" | custom-call | bytes 67108864 | tf_op jit(solution)/shard_map/pallas_call | solution.py:645
  94.0 2.7 %shard_map.94 = (bf16[128,1024]{1,0:T(8,128)(2,1)}, bf16[128,4096]{1,0:T(8,128)(2,1)}, f32[512,512]{1,0:T(8,128)}, bf16[128,128]{1,0:T(8,128)(2,1)}) custom-call(bf16[128,1024]{1,0:T(8,128)(2,1)} %get-tuple-element.12.refs_0_, bf16[128,4096]{1,0:T(8,128)(2,1)} %get-tuple-element.13.refs_1_, f32[512,512]{1,0:T(8,128)} %get-tuple-element.14.refs_2_, ...), custom_call_target="tpu_custom_call" | custom-call | tf_op jit(solution)/shard_map/pallas_call | solution.py:726

commit v7 on v6

--- a/solution.py
+++ b/solution.py
@@ -8,7 +8,7 @@
 STAT_DECAY = 0.8
 NORM_EPSILON = 1e-06
 MESH = pl.DeviceIdType.MESH
-VMEM_LIMIT = 60 * 1024 * 1024
+VMEM_LIMIT = 48 * 1024 * 1024
 
 NX, NY, NZ = 4, 4, 8
 BS = 512
@@ -427,7 +427,6 @@
     for d in (1, 3):
         wy_from(d, 0).wait_recv()
         wf(d, half_from(d, lax.rem(y + 4 - d, 4))).start()
-        wy(d, 1, y).start()
         wc(d, early_part(d, core)).start()
 
     local[1].wait()
@@ -474,9 +473,9 @@
     def products(i):
         band = weight[i].reshape(1024, 1024)
         here = jnp.dot(tok_own[:, 1024 * i : 1024 * i + 1024], band, preferred_element_type=jnp.float32)
-        if i:
+        if i != 1:
             here = here + projected_sum[...]
-        if i < 3:
+        if i != 3:
             projected_sum[...] = here
         else:
             projected[...] = here.astype(jnp.bfloat16)
@@ -527,6 +526,16 @@
         for d in (8, 7, 9, 6, 10, 5, 11, 4, 12, 3, 13, 2, 14, 1, 15):
             s_copy(d).start()
         spread[group] = chunks[group]
+
+    for d in (1, 3):
+        wf(d, half_from(d, to_y(2))).wait_recv()
+    wc(2, rows_from(2, core)).start()
+    for d in (1, 3):
+        wf(d, half_from(d, y)).wait_send()
+        wy(d, 1, y).start()
+
+    @pl.when(side == 1)
+    def _():
         for d in range(1, 8):
             e_copy(d).wait_recv()
         total = jnp.zeros((8, 128), jnp.float32)
@@ -537,13 +546,6 @@
             n_copy(d).start()
 
 
-    for d in (1, 3):
-        wy_from(d, 1).wait_recv()
-        wc(d + 3, late_part(d, core)).start()
-    for d in (1, 3):
-        wf(d, half_from(d, to_y(2))).wait_recv()
-    wc(2, rows_from(2, core)).start()
-
     @pl.when(side == 1)
     def _():
         for d in range(1, NB):
@@ -566,10 +568,15 @@
     wc(2, rows_from(2, 1 - core)).wait()
     for d in (1, 3):
         wc(d, early_part(d, 1 - core)).wait()
+    products(1)
+    products(2)
+    for d in (1, 3):
+        wy_from(d, 1).wait_recv()
+        wc(d + 3, late_part(d, core)).start()
+    for d in (1, 3):
         wc(d + 3, late_part(d, 1 - core)).wait()
-
-    for i in range(4):
-        products(i)
+    products(0)
+    products(3)
 
     for dp, fsdp, i, q in sources:
         @pl.when(away(dp, fsdp))
@@ -633,22 +640,21 @@
     for d in (1, 3):
         wy(d, 0, y).wait_send()
         wy(d, 1, y).wait_send()
-        wf(d, half_from(d, y)).wait_send()
 
 
 def update(table, tokens, upstream, shard, stats_prev, root_prev):
     dma = pltpu.SemaphoreType.DMA
     f32, b16 = jnp.float32, jnp.bfloat16
-    anywhere, vmem = pl.BlockSpec(memory_space=pl.ANY), pl.BlockSpec(memory_space=pltpu.VMEM)
+    anywhere, vmem = pl.BlockSpec(memory_space=pltpu.HBM), pl.BlockSpec(memory_space=pltpu.VMEM)
     rows = tokens.shape[0]
     square = pltpu.VMEM((BS, BS), f32)
     return pl.pallas_call(
         update_kernel,
         out_shape=(
-            jax.ShapeDtypeStruct((rows, 1024), b16),
-            jax.ShapeDtypeStruct((rows, 4096), b16),
-            jax.ShapeDtypeStruct((BS, BS), f32),
-            jax.ShapeDtypeStruct((128, 128), b16),
+            pltpu.VMEM((rows, 1024), b16),
+            pltpu.VMEM((rows, 4096), b16),
+            pltpu.VMEM((BS, BS), f32),
+            pltpu.VMEM((128, 128), b16),
         ),
         in_specs=[pl.BlockSpec(memory_space=pltpu.SMEM)] + [anywhere] * 5,
         out_specs=(vmem,) * 4,
@@ -703,34 +709,33 @@
             collective_id=0, has_side_effects=True, vmem_limit_bytes=VMEM_LIMIT
         ),
         cost_estimate=pl.CostEstimate(flops=0, bytes_accessed=64 << 20, transcendentals=0),
-    )(table, tokens, upstream, shard, stats_prev, root_prev)
+    )(
+        *(
+            pltpu.with_memory_space_constraint(a, pltpu.HBM)
+            for a in (table, tokens, upstream, shard, stats_prev, root_prev)
+        )
+    )
 
 
 def settle_kernel(*refs):
-    n = (len(refs) - 2) // 3
-    given, taken, held, come, gone = refs[:n], refs[n : 2 * n], refs[2 * n : 3 * n], refs[-2], refs[-1]
-    reads = [pltpu.make_async_copy(given[i], held[i], come.at[i]) for i in range(n)]
-    writes = [pltpu.make_async_copy(held[i], taken[i], gone.at[i]) for i in range(n)]
-    for copy in reads:
+    n = len(refs) // 2
+    copies = [pltpu.make_async_copy(refs[i], refs[n + i], refs[-1].at[i]) for i in range(n)]
+    for copy in copies:
         copy.start()
-    for i in range(n):
-        reads[i].wait()
-        writes[i].start()
-    for copy in writes:
+    for copy in copies:
         copy.wait()
 
 
 def settle(*arrays):
-    anywhere = pl.BlockSpec(memory_space=pl.ANY)
     n = len(arrays)
     return pl.pallas_call(
         settle_kernel,
-        out_shape=tuple(jax.ShapeDtypeStruct(a.shape, a.dtype) for a in arrays),
-        in_specs=[anywhere] * n,
-        out_specs=(anywhere,) * n,
-        scratch_shapes=[pltpu.VMEM(a.shape, a.dtype) for a in arrays] + [pltpu.SemaphoreType.DMA((n,))] * 2,
-        compiler_params=pltpu.CompilerParams(vmem_limit_bytes=VMEM_LIMIT),
-    )(*arrays)
+        out_shape=tuple(pltpu.HBM(a.shape, a.dtype) for a in arrays),
+        in_specs=[pl.BlockSpec(memory_space=pltpu.VMEM)] * n,
+        out_specs=(pl.BlockSpec(memory_space=pltpu.HBM),) * n,
+        scratch_shapes=[pltpu.SemaphoreType.DMA((n,))],
+        compiler_params=pltpu.CompilerParams(vmem_limit_bytes=16 * 1024 * 1024),
+    )(*(pltpu.with_memory_space_constraint(a, pltpu.VMEM) for a in arrays))
 
 
 def local(tokens, upstream, weight, owner_table, stats_prev, roots_prev):

time: 98.7 us -> 95.5 us (0.968); the launches traced: 96.8 us -> 94.8 us
  Pallas kernels: 96 us -> 94 us
    pallas_call x2, Pallas kernels: 96 us -> 94 us  [the longest x1 92.5 us: update(): pl.pallas_call(update_kernel, out_shape=(pltpu.VMEM((rows, 1024), b16), p...]
where the time goes in v7:
time: 95.5 us; the launch traced here: 94.8 us
  Pallas kernels  94 us (98%)
    pallas_call x1, Pallas kernels, update(): pl.pallas_call(update_kernel, out_shape=(pltpu.VMEM((rows, 1024), b16), p...  92.5 us

profile of v7, /device:TPU:8, one launch (start us, length us, event | category | flops | bytes accessed | tf_op | source)
XLA Modules:
  0.0 94.8 jit_solution(14052797391083198953)
XLA Ops:
  0.6 92.5 %shard_map.93 = (bf16[128,1024]{1,0:T(8,128)(2,1)S(1)}, bf16[128,4096]{1,0:T(8,128)(2,1)S(1)}, f32[512,512]{1,0:T(8,128)S(1)}, bf16[128,128]{1,0:T(8,128)(2,1)S(1)}) custom-call(s32[16]{0:T(128)} %table.1, bf16[128,4096]{1,0:T(8,128)(2,1)} %tok.1, bf16[128,1024]{1,0:T(8,128)(2,1)} %ups.1, bf16[128,1024]{1,0:T(8,128)(2,1)} %shard.1, f32[512,512]{1,0:T(8,128)} %bitcast.3, ...), custom_call_target="tpu_custom_call" | custom-call | bytes 67108864 | tf_op jit(solution)/shard_map/pallas_call | solution.py:651
  93.2 1.4 %shard_map.94 = (bf16[128,1024]{1,0:T(8,128)(2,1)}, bf16[128,4096]{1,0:T(8,128)(2,1)}, f32[512,512]{1,0:T(8,128)}, bf16[128,128]{1,0:T(8,128)(2,1)}) custom-call(bf16[128,1024]{1,0:T(8,128)(2,1)S(1)} %get-tuple-element.12.refs_0_, bf16[128,4096]{1,0:T(8,128)(2,1)S(1)} %get-tuple-element.13.refs_1_, f32[512,512]{1,0:T(8,128)S(1)} %get-tuple-element.14.refs_2_, ...), custom_call_target="tpu_custom_call" | custom-call | tf_op jit(solution)/shard_map/pallas_call | solution.py:731
